TPU v7x, 32 devices: a whole 2x2x4 slice. The times are simulated.
32 devices in a mesh: seq: 16 (over z, y, x), tp: 2 (over core).
Axes of the slice: x: 2, y: 2, z: 4, core: 2. Of those that a mesh axis runs over, the one named last changes fastest.
Arguments:
- tokens: float32 [4096, 768], P('seq'), may hold values from -6 to 6
- cotangent: float32 [4096, 768], P('seq'), may hold values from -6 to 6
- norm1_gain: float32 [768], replicated, may hold values from 0.5 to 1.5
- norm1_bias: float32 [768], replicated, may hold values from -1.75 to 1.75
- query_weight: float32 [768, 768], P(None, 'tp'), may hold values from -0.21875 to 0.21875
- query_bias: float32 [768], P('tp'), may hold values from -1.75 to 1.75
- key_weight: float32 [768, 768], P(None, 'tp'), may hold values from -0.21875 to 0.21875
- key_bias: float32 [768], P('tp'), may hold values from -1.75 to 1.75
- value_weight: float32 [768, 768], P(None, 'tp'), may hold values from -0.21875 to 0.21875
- value_bias: float32 [768], P('tp'), may hold values from -1.75 to 1.75
- shift_kernel: float32 [4, 768], P(None, 'tp'), may hold values from -3 to 3
- log_step: float32 [768], P('tp'), as said below
- state_rate: float32 [64, 768], P(None, 'tp'), may hold values from 1 to 64
- state_out: float32 [64, 768], P(None, 'tp'), may hold values from -0.75 to 0.75
- skip_gain: float32 [768], P('tp'), may hold values from -4 to 4
- out_weight: float32 [768, 768], P('tp'), may hold values from -0.21875 to 0.21875
- out_bias: float32 [768], replicated, may hold values from -1.75 to 1.75
- norm2_gain: float32 [768], replicated, may hold values from 0.5 to 1.5
- norm2_bias: float32 [768], replicated, may hold values from -1.75 to 1.75
- up_weight: float32 [768, 3072], P(None, 'tp'), may hold values from -0.21875 to 0.21875
- up_bias: float32 [3072], P('tp'), may hold values from -1.75 to 1.75
- down_weight: float32 [3072, 768], P('tp'), may hold values from -0.109375 to 0.109375
- down_bias: float32 [768], replicated, may hold values from -1.75 to 1.75
Outputs:
- block_out: float32 [4096, 768], P('seq')
- input_grad: float32 [4096, 768], P('seq')
- grad_norm1_gain: float32 [768], replicated
- grad_norm1_bias: float32 [768], replicated
- grad_query_weight: float32 [768, 768], P(None, 'tp')
- grad_query_bias: float32 [768], P('tp')
- grad_key_weight: float32 [768, 768], P(None, 'tp')
- grad_key_bias: float32 [768], P('tp')
- grad_value_weight: float32 [768, 768], P(None, 'tp')
- grad_value_bias: float32 [768], P('tp')
- grad_shift_kernel: float32 [4, 768], P(None, 'tp')
- grad_log_step: float32 [768], P('tp')
- grad_state_rate: float32 [64, 768], P(None, 'tp')
- grad_state_out: float32 [64, 768], P(None, 'tp')
- grad_skip_gain: float32 [768], P('tp')
- grad_out_weight: float32 [768, 768], P('tp')
- grad_out_bias: float32 [768], replicated
- grad_norm2_gain: float32 [768], replicated
- grad_norm2_bias: float32 [768], replicated
- grad_up_weight: float32 [768, 3072], P(None, 'tp')
- grad_up_bias: float32 [3072], P('tp')
- grad_down_weight: float32 [3072, 768], P('tp')
- grad_down_bias: float32 [768], replicated
Inputs may be any that keep to these rules, and one draw needn't show every extreme that they name: `log_step`: uniform between log(0.05 / 2048) and log(0.005).
All inputs are finite; a program needn't handle non-finite values.
Results may differ from a plain program's by a relative error of at most 0.0003.
Values sent between devices are 32-bit elements; how exact they have to be, the bound alone decides.
A program may use at most 256 MiB of HBM per device.

v0:
```python
import functools

import jax
import jax.numpy as jnp
from jax import lax
from jax.experimental import pallas as pl
from jax.experimental.pallas import tpu as pltpu
from jax.sharding import PartitionSpec as P

SHIFT = 4
SEQS = 2
STATE = 64
LANES = 128
CHUNK = 32
PIECE_ROWS = 24
LAG = 2
GELU_SCALE = (2.0 / 3.141592653589793) ** 0.5

EPSILON = 1e-05
F32 = jnp.float32
PRECISION = lax.Precision.HIGH


def shape(*dims):
    return jax.ShapeDtypeStruct(dims, F32)


def fold_states(values):
    return jnp.sum(values.reshape(STATE // 8, 8, LANES), axis=0)


def cut(block):
    return pl.ds(block * LANES, LANES)


class Sequence:
    def __init__(self, span, backward):
        self.me = lax.axis_index("seq")
        self.span = span
        self.place = lax.rem(self.me, span)
        self.start = self.me - self.place
        self.groups = span // 4
        self.quarter, self.group = lax.rem(self.place, 4), self.place // 4
        if backward:
            self.rank, self.turn = 3 - self.quarter, self.groups - 1 - self.group
        else:
            self.rank, self.turn = self.quarter, self.group
        self.backward = backward

    def greet(self, other_core=None):
        barrier = pltpu.get_barrier_semaphore()
        for k in range(1, self.span):
            peer = self.start + lax.rem(self.place + k, self.span)
            pl.semaphore_signal(barrier, inc=1, device_id={"seq": peer}, device_id_type=pl.DeviceIdType.MESH)
        if other_core is not None:
            pl.semaphore_signal(barrier, inc=1, device_id={"tp": other_core}, device_id_type=pl.DeviceIdType.MESH)
        pl.semaphore_wait(barrier, self.span - 1 + (other_core is not None))

    def remote(self, source, target, send, recv, peer, core=None):
        return pltpu.make_async_remote_copy(
            src_ref=source,
            dst_ref=target,
            send_sem=send,
            recv_sem=recv,
            device_id={"seq": peer} if core is None else {"tp": core},
            device_id_type=pl.DeviceIdType.MESH,
        )

    def end_copy(self, b, k, ends_ref, sems):
        other = lax.rem(self.quarter + k, 4)
        peer = self.me - self.quarter + other
        ref = ends_ref.at[self.rank, :, cut(b)]
        return self.remote(ref, ref, sems[0].at[b, k - 1], sems[1].at[b, k - 1], peer)

    def total_copy(self, b, k, totals_ref, sems):
        peer = self.me - 4 * k if self.backward else self.me + 4 * k
        ref = totals_ref.at[self.turn, :, cut(b)]
        return self.remote(ref, ref, sems[2].at[b, k - 1], sems[3].at[b, k - 1], peer)

    def send_end(self, b, end, ends_ref, sems):
        ends_ref[self.rank, :, cut(b)] = end
        for k in range(1, 4):
            self.end_copy(b, k, ends_ref, sems).start()

    def group_total(self, b, decay, ends_ref, totals_ref, sems):
        for k in range(1, 4):
            self.end_copy(b, k, ends_ref, sems).wait_recv()
        before = jnp.zeros_like(decay)
        total = ends_ref[0, :, cut(b)]
        for r in range(3):
            before = jnp.where(self.rank > r, before * decay + ends_ref[r, :, cut(b)], before)
            total = total * decay + ends_ref[r + 1, :, cut(b)]
        if self.groups > 1:
            totals_ref[self.turn, :, cut(b)] = total
            for k in range(1, self.groups):
                pl.when(self.turn + k < self.groups)(lambda: self.total_copy(b, k, totals_ref, sems).start())
        return before

    def carried(self, b, decay, before, totals_ref, sems):
        if self.groups == 1:
            return before
        square = decay * decay
        fourth = square * square
        carry = jnp.zeros_like(decay)
        for h in range(self.groups - 1):
            for k in range(1, self.groups - h):
                pl.when(self.turn == h + k)(lambda: self.total_copy(b, k, totals_ref, sems).wait_recv())
        for h in range(self.groups - 1):
            carry = jnp.where(self.turn > h, carry * fourth + totals_ref[h, :, cut(b)], carry)
        for r in range(3):
            carry = jnp.where(self.rank > r, carry * decay, carry)
        return before + carry

    def drain(self, blocks, ends_ref, totals_ref, sems):
        for b in range(blocks):
            for k in range(1, 4):
                self.end_copy(b, k, ends_ref, sems).wait_send()
            for k in range(1, self.groups):
                pl.when(self.turn + k < self.groups)(lambda: self.total_copy(b, k, totals_ref, sems).wait_send())


def mixer_kernel(
    span, query_ref, key_ref, value_ref, taps_ref, skip_ref, decay_ref, out_coef_ref, device_decay_ref,
    gated_ref, out_ref, mixed_ref, shifted_ref, starts_ref, halo_ref,
    keys_ref, rows_ref, part_ref, ends_ref, totals_ref, end_send, end_recv, total_send, total_recv, halo_send, halo_recv
):
    tokens, width = key_ref.shape
    blocks = width // LANES
    seq = Sequence(span, False)
    sems = (end_send, end_recv, total_send, total_recv)
    keys_ref[pl.ds(8, tokens), :] = key_ref[...]
    seq.greet()

    def halo_copy(peer):
        return seq.remote(key_ref.at[pl.ds(tokens - 8, 8)], halo_ref, halo_send.at[0], halo_recv.at[0], peer)

    first, last = seq.place == 0, seq.place == span - 1
    pl.when(jnp.logical_not(last))(lambda: halo_copy(seq.me + 1).start())

    def mix(start, count):
        total = taps_ref[0:1, :] * keys_ref[pl.ds(8 + start, count), :]
        for j in range(1, SHIFT):
            total = total + taps_ref[j : j + 1, :] * keys_ref[pl.ds(8 + start - j, count), :]
        shifted_ref[pl.ds(start, count), :] = total
        mixed = total * value_ref[pl.ds(start, count), :]
        mixed_ref[pl.ds(start, count), :] = mixed
        for b in range(blocks):
            rows_ref[b, pl.ds(start, count), :] = mixed[:, b * LANES : (b + 1) * LANES]

    mix(8, tokens - 8)

    @pl.when(first)
    def _():
        halo_ref[...] = jnp.zeros_like(halo_ref)

    @pl.when(jnp.logical_not(first))
    def _():
        halo_copy(seq.me + 1).wait_recv()

    keys_ref[pl.ds(0, 8), :] = halo_ref[...]
    mix(0, 8)
    for b in range(blocks):
        decay, out_coef = decay_ref[:, cut(b)], out_coef_ref[:, cut(b)]

        def scan(k, state, b=b, decay=decay, out_coef=out_coef):
            starts_ref[k, :, cut(b)] = state
            base = pl.multiple_of(k * CHUNK, CHUNK)
            for j in range(CHUNK):
                state = decay * state + rows_ref[b, pl.ds(base + j, 1), :]
                part_ref[j] = fold_states(out_coef * state)
            out_ref[pl.ds(base, CHUNK), cut(b)] = jnp.sum(part_ref[...], axis=1)
            return state

        seq.send_end(b, lax.fori_loop(0, tokens // CHUNK, scan, jnp.zeros_like(decay)), ends_ref, sems)
    befores = [seq.group_total(b, device_decay_ref[:, cut(b)], ends_ref, totals_ref, sems) for b in range(blocks)]
    for b in range(blocks):
        decay, out_coef = decay_ref[:, cut(b)], out_coef_ref[:, cut(b)]
        skip = skip_ref[:, cut(b)]

        def carry(k, state, b=b, decay=decay, out_coef=out_coef, skip=skip):
            starts_ref[k, :, cut(b)] = starts_ref[k, :, cut(b)] + state
            base = pl.multiple_of(k * CHUNK, CHUNK)
            for j in range(CHUNK):
                state = decay * state
                part_ref[j] = fold_states(out_coef * state)
            rows = pl.ds(base, CHUNK)
            out = out_ref[rows, cut(b)] + jnp.sum(part_ref[...], axis=1) + skip * mixed_ref[rows, cut(b)]
            out_ref[rows, cut(b)] = out
            gated_ref[rows, cut(b)] = query_ref[rows, cut(b)] * out
            return state

        incoming = seq.carried(b, device_decay_ref[:, cut(b)], befores[b], totals_ref, sems)
        lax.fori_loop(0, tokens // CHUNK, carry, incoming)
    seq.drain(blocks, ends_ref, totals_ref, sems)
    pl.when(jnp.logical_not(last))(lambda: halo_copy(seq.me + 1).wait_send())


def dot(left, right, left_axis, right_axis):
    return lax.dot_general(
        left, right, (((left_axis,), (right_axis,)), ((), ())), precision=PRECISION, preferred_element_type=F32
    )


def over_tokens(values):
    return jnp.sum(values, axis=0, keepdims=True)


def over_features(values):
    return jnp.mean(values, axis=1, keepdims=True)


class Share:
    def __init__(self, seq, source_ref, target_ref, send, recv, peer, core, other_core):
        self.source_ref, self.target_ref, self.send, self.recv = source_ref, target_ref, send, recv
        self.seq, self.peer, self.core, self.other_core = seq, peer, core, other_core
        size = source_ref.shape[0] // 2
        self.mine = pl.ds(pl.multiple_of(core * size, 8), size)

    def across(self):
        return self.seq.remote(
            self.source_ref.at[self.mine], self.target_ref.at[self.mine], self.send.at[0], self.recv.at[0], self.peer
        )

    def between(self):
        ref = self.target_ref.at[self.mine]
        return self.seq.remote(ref, ref, self.send.at[1], self.recv.at[1], self.seq.me, self.other_core)

    def relay(self):
        self.across().wait_recv()
        self.between().start()

    def finish(self):
        self.between().wait_recv()
        self.across().wait_send()
        self.between().wait_send()


def layer_kernel(
    span,
    gated_ref, tokens_ref, cotangent_ref, out_weight_ref, out_bias_ref, gain_ref, bias_ref, up_hbm, up_bias_ref, down_hbm,
    down_bias_ref, query_ref, key_ref, value_ref, halo_ref, out_ref, mixed_ref, shifted_ref, starts_ref, taps_ref,
    skip_ref, decay_ref, out_coef_ref, device_decay_ref, normed1_ref, in_coef_ref, coef_rate_ref, rate_ref, step_ref,
    block_out_ref, middle_grad_ref, query_grad_ref, key_grad_ref, value_grad_ref, small_ref, down_half_ref, up_half_ref,
    normed1_x_ref, narrow_x_ref, wide_y_ref, narrow_y_ref,
    up_ref, down_ref, active_ref, pre_grad_ref, normed_ref, scaled_ref, middle_ref, merged_ref, merged_other_ref,
    feed_ref, feed_other_ref, normed_grad_ref, normed_grad_other_ref,
    active_peer_ref, pre_grad_peer_ref, cotangent_peer_ref, normed_peer_ref,
    gated_grad_ref, grad_ref, rows_ref, grad_rows_ref, keys_ref, shifted_grad_ref, head_ref, part_ref, state_ref,
    coef_ref, slope_ref, ends_ref, totals_ref,
    end_send, end_recv, total_send, total_recv, halo_send, halo_recv,
    load_sem, core_send, core_recv, half_send, half_recv, share_send, share_recv
):
    tokens, width = key_ref.shape
    hidden = up_ref.shape[1]
    hidden_half = hidden // 2
    blocks = width // LANES
    chunks = tokens // CHUNK
    seq = Sequence(span, True)
    sems = (end_send, end_recv, total_send, total_recv)
    x, y = lax.rem(seq.me, 2), lax.rem(seq.me // 2, 2)
    x_peer, y_peer = seq.me + 1 - 2 * x, seq.me + 2 - 4 * y
    core = lax.axis_index("tp")
    other_core = 1 - core
    loads = [
        pltpu.make_async_copy(source, target, load_sem.at[n])
        for n, (source, target) in enumerate(((up_hbm, up_ref), (down_hbm, down_ref)))
    ]
    for load in loads:
        load.start()
    seq.greet(other_core)

    def core_copy(n, source, target):
        return seq.remote(source, target, core_send.at[n], core_recv.at[n], seq.me, other_core)

    cotangent_share = Share(
        seq, cotangent_ref, cotangent_peer_ref, share_send.at[0], share_recv.at[0], x_peer, core, other_core
    )
    normed_share = Share(
        seq, normed_ref, normed_peer_ref, share_send.at[1], share_recv.at[1], y_peer, core, other_core
    )
    normed1_share = Share(
        seq, normed1_ref, normed1_x_ref, share_send.at[2], share_recv.at[2], x_peer, core, other_core
    )
    wide_shares = [
        Share(seq, source, wide_y_ref, share_send.at[3], share_recv.at[3], y_peer, core, other_core)
        for source in (middle_grad_ref, normed1_ref)
    ]

    def narrow_copies():
        return (
            seq.remote(key_grad_ref, narrow_x_ref, half_send.at[2], half_recv.at[2], x_peer),
            seq.remote(query_grad_ref, narrow_x_ref, half_send.at[2], half_recv.at[2], x_peer),
            seq.remote(gated_ref, narrow_y_ref, half_send.at[3], half_recv.at[3], y_peer),
            seq.remote(value_grad_ref, narrow_y_ref, half_send.at[3], half_recv.at[3], y_peer),
        )

    cotangent_share.across().start()
    normed1_share.across().start()
    pl.when(y == 0)(lambda: narrow_copies()[2].start())
    pl.when(y == 1)(lambda: wide_shares[1].across().start())

    small_ref[...] = jnp.zeros_like(small_ref)

    def put(k, row):
        small_ref[1, pl.ds(STATE // 4 + k // 2, 1), pl.ds(k % 2 * width, width)] = row

    top = tokens // 2
    merged_copies = []
    for n in range(2):
        rows = pl.ds(n * top, top)
        merged_ref[rows, :] = dot(gated_ref[rows, :], out_weight_ref[...], 1, 0)
        copy = core_copy(n, merged_ref.at[rows], merged_other_ref.at[rows])
        copy.start()
        merged_copies.append(copy)
    spreads = []
    for n, copy in enumerate(merged_copies):
        rows = pl.ds(n * top, top)
        copy.wait_recv()
        middle = tokens_ref[rows, :] + (merged_ref[rows, :] + merged_other_ref[rows, :]) + out_bias_ref[...]
        centered = middle - over_features(middle)
        inverse = lax.rsqrt(over_features(centered * centered) + EPSILON)
        scaled = centered * inverse
        middle_ref[rows, :] = middle
        scaled_ref[rows, :] = scaled
        normed_ref[rows, :] = scaled * gain_ref[...] + bias_ref[...]
        spreads.append(inverse)
    normed_share.across().start()

    for load in loads:
        load.wait()
    for n in range(2):
        part = pl.ds(n * hidden_half, hidden_half)
        pre = dot(normed_ref[...], up_ref[:, part], 1, 0) + up_bias_ref[:, part]
        square = pre * pre
        curve = jnp.tanh(GELU_SCALE * (pre + 0.044715 * (square * pre)))
        active = 0.5 * pre * (1.0 + curve)
        active_ref[n] = active
        slope = 0.5 * (1.0 + curve) + 0.5 * pre * (1.0 - curve * curve) * (
            GELU_SCALE * (1.0 + 3 * 0.044715 * square)
        )
        pre_grad = dot(cotangent_ref[...], down_ref[part, :], 1, 1) * slope
        pre_grad_ref[n] = pre_grad
        small_ref[0, pl.ds(STATE // 4 + 6 + n, 1), :] = over_tokens(pre_grad)
        normed_grad = dot(pre_grad, up_ref[:, part], 1, 1)
        if n == 0:
            normed_grad_ref[...] = normed_grad
        else:
            normed_grad_ref[...] = normed_grad_ref[...] + normed_grad
    normed_grad_copy = core_copy(2, normed_grad_ref, normed_grad_other_ref)
    normed_grad_copy.start()
    for n in range(2):
        part = pl.ds(n * hidden_half, hidden_half)
        feed = dot(active_ref[n], down_ref[part, :], 1, 0)
        if n == 0:
            feed_ref[...] = feed
        else:
            feed_ref[...] = feed_ref[...] + feed
    feed_copy = core_copy(3, feed_ref, feed_other_ref)
    feed_copy.start()
    cotangent_share.relay()
    normed1_share.relay()
    normed_share.relay()
    normed_grad_copy.wait_recv()
    for n in range(2):
        rows = pl.ds(n * top, top)
        normed_grad = normed_grad_ref[rows, :] + normed_grad_other_ref[rows, :]
        scaled = scaled_ref[rows, :]
        scaled_grad = normed_grad * gain_ref[...]
        centered = scaled_grad - over_features(scaled_grad) - scaled * over_features(scaled_grad * scaled)
        middle_grad = cotangent_ref[rows, :] + spreads[n] * centered
        middle_grad_ref[rows, :] = middle_grad
        sums = (normed_grad * scaled, normed_grad, middle_grad, cotangent_ref[rows, :])
        for k, values in enumerate(sums):
            row = pl.ds(STATE // 4 + 2 + k, 1)
            if n == 0:
                small_ref[0, row, :] = over_tokens(values)
            else:
                small_ref[0, row, :] = small_ref[0, row, :] + over_tokens(values)
        gated_grad_ref[rows, :] = dot(middle_grad, out_weight_ref[...], 1, 1)

    grad = gated_grad_ref[...] * query_ref[...]
    grad_ref[...] = grad
    for b in range(blocks):
        grad_rows_ref[b] = grad[:, b * LANES : (b + 1) * LANES]
        rows_ref[b] = mixed_ref[:, cut(b)]
    for b in range(blocks):
        decay = decay_ref[:, cut(b)]

        def end(i, adjoint, b=b, decay=decay):
            base = pl.multiple_of((chunks - 1 - i) * CHUNK, CHUNK)
            for j in range(CHUNK - 1, -1, -1):
                adjoint = decay * adjoint + grad_rows_ref[b, pl.ds(base + j, 1), :]
            return adjoint

        seq.send_end(b, lax.fori_loop(0, chunks, end, jnp.zeros_like(decay)), ends_ref, sems)
    query_grad = gated_grad_ref[...] * out_ref[...]
    query_grad_ref[...] = query_grad
    keys_ref[pl.ds(0, 8), :] = halo_ref[...]
    keys_ref[pl.ds(8, tokens), :] = key_ref[...]
    put(0, over_tokens(grad_ref[...] * mixed_ref[...]))
    put(5, over_tokens(query_grad))
    feed_copy.wait_recv()
    block_out_ref[...] = middle_ref[...] + (feed_ref[...] + feed_other_ref[...]) + down_bias_ref[...]

    def half_product(result_ref, left_ref, right_ref, first):
        size = width

        def tile(i, _):
            part = pl.ds(pl.multiple_of(i * size, size), size)
            product = dot(left_ref[:, part], right_ref[...], 0, 0)
            result_ref[part, :] = product if first else result_ref[part, :] + product
            return 0

        lax.fori_loop(0, result_ref.shape[0] // size, tile, 0)

    befores = [seq.group_total(b, device_decay_ref[:, cut(b)], ends_ref, totals_ref, sems) for b in range(blocks)]
    half_product(down_half_ref, active_ref.at[x], cotangent_ref, True)
    incoming = [seq.carried(b, device_decay_ref[:, cut(b)], befores[b], totals_ref, sems) for b in range(blocks)]

    def half_copies():
        return (
            seq.remote(active_ref.at[1 - x], active_peer_ref, half_send.at[0], half_recv.at[0], x_peer),
            seq.remote(pre_grad_ref.at[1 - y], pre_grad_peer_ref, half_send.at[1], half_recv.at[1], y_peer),
        )

    for copy in half_copies():
        copy.start()
    pl.when(y == 0)(lambda: wide_shares[0].across().start())
    pl.when(x == 1)(lambda: narrow_copies()[1].start())

    def state_sums():
        quarter = STATE // 4
        for p in range(4):
            rows = pl.ds(p * quarter, quarter)
            coef = coef_ref[rows, :]
            rate_grad = coef_rate_ref[rows, :] * coef - decay_ref[rows, :] * out_coef_ref[rows, :] * slope_ref[rows, :]
            step_grad = over_tokens(rate_ref[rows, :] * rate_grad)
            put(8, step_grad if p == 0 else small_ref[1, pl.ds(quarter + 4, 1), pl.ds(0, width)] + step_grad)
            small_ref[p, pl.ds(0, quarter), pl.ds(0, width)] = step_ref[...] * rate_grad
            small_ref[p, pl.ds(0, quarter), pl.ds(width, width)] = in_coef_ref[rows, :] * coef

    for b in range(blocks):
        decay, out_coef = decay_ref[:, cut(b)], out_coef_ref[:, cut(b)]
        skip = skip_ref[:, cut(b)]
        coef_ref[:, cut(b)] = jnp.zeros_like(decay)
        slope_ref[:, cut(b)] = jnp.zeros_like(decay)

        def chunk(i, adjoint, b=b, decay=decay, out_coef=out_coef, skip=skip):
            k = chunks - 1 - i
            base = pl.multiple_of(k * CHUNK, CHUNK)
            state = starts_ref[k, :, cut(b)]
            for j in range(CHUNK):
                state_ref[j] = state
                state = decay * state + rows_ref[b, pl.ds(base + j, 1), :]
            coef, slope = coef_ref[:, cut(b)], slope_ref[:, cut(b)]
            for j in range(CHUNK - 1, -1, -1):
                adjoint = decay * adjoint + grad_rows_ref[b, pl.ds(base + j, 1), :]
                part_ref[j] = fold_states(out_coef * adjoint)
                coef = coef + adjoint * rows_ref[b, pl.ds(base + j, 1), :]
                slope = slope + adjoint * state_ref[j]
            coef_ref[:, cut(b)] = coef
            slope_ref[:, cut(b)] = slope
            rows = pl.ds(base, CHUNK)
            grad_mixed = jnp.sum(part_ref[...], axis=1) + skip * grad_ref[rows, cut(b)]
            shifted_grad_ref[rows, cut(b)] = grad_mixed * value_ref[rows, cut(b)]
            value_grad_ref[rows, cut(b)] = grad_mixed * shifted_ref[rows, cut(b)]
            return adjoint

        lax.fori_loop(0, chunks, chunk, incoming[b])

    def halo_copy():
        return seq.remote(
            shifted_grad_ref.at[pl.ds(0, 8)], head_ref, halo_send.at[0], halo_recv.at[0], seq.me - 1
        )

    first, last = seq.place == 0, seq.place == span - 1
    pl.when(jnp.logical_not(first))(lambda: halo_copy().start())
    for j in range(SHIFT):
        put(1 + j, over_tokens(shifted_grad_ref[pl.ds(0, tokens), :] * keys_ref[pl.ds(8 - j, tokens), :]))
    pl.when(y == 1)(lambda: narrow_copies()[3].start())
    put(7, over_tokens(value_grad_ref[...]))
    half_product(up_half_ref, normed_ref, pre_grad_ref.at[y], True)

    @pl.when(last)
    def _():
        head_ref[...] = jnp.zeros_like(head_ref)

    @pl.when(jnp.logical_not(last))
    def _():
        halo_copy().wait_recv()

    shifted_grad_ref[pl.ds(tokens, 8), :] = head_ref[...]
    key_grad = taps_ref[0:1, :] * shifted_grad_ref[pl.ds(0, tokens), :]
    for j in range(1, SHIFT):
        key_grad = key_grad + taps_ref[j : j + 1, :] * shifted_grad_ref[pl.ds(j, tokens), :]
    key_grad_ref[...] = key_grad
    put(6, over_tokens(key_grad))
    pl.when(x == 0)(lambda: narrow_copies()[0].start())
    state_sums()

    cotangent_share.finish()
    normed_share.finish()
    for copy in half_copies():
        copy.wait()
    half_product(down_half_ref, active_peer_ref, cotangent_peer_ref, False)
    half_product(up_half_ref, normed_peer_ref, pre_grad_peer_ref, False)
    wide_shares[0].relay()
    normed1_share.finish()
    wide_shares[0].finish()
    for copy in narrow_copies()[::2]:
        copy.wait()
    for copy in merged_copies + [normed_grad_copy, feed_copy]:
        copy.wait_send()
    seq.drain(blocks, ends_ref, totals_ref, sems)
    pl.when(jnp.logical_not(first))(lambda: halo_copy().wait_send())


def mixer_call(kernel, span, args, outs, scratch, width, collective_id, name, more_sems=(), in_hbm=(), megabytes=16):
    blocks, groups = width // LANES, span // 4
    scratch = [pltpu.VMEM(dims, F32) for dims in scratch]
    scratch += [pltpu.VMEM((4, STATE, width), F32), pltpu.VMEM((groups, STATE, width), F32)]
    sems = [(blocks, 3), (blocks, 3), (blocks, max(1, groups - 1)), (blocks, max(1, groups - 1)), (1,), (1,), *more_sems]
    return pl.pallas_call(
        functools.partial(kernel, span),
        in_specs=[pl.BlockSpec(memory_space=pltpu.HBM if n in in_hbm else pltpu.VMEM) for n in range(len(args))],
        out_specs=[pl.BlockSpec(memory_space=pltpu.VMEM)] * len(outs),
        out_shape=outs,
        scratch_shapes=scratch + [pltpu.SemaphoreType.DMA(dims) for dims in sems],
        compiler_params=pltpu.CompilerParams(
            collective_id=collective_id, has_side_effects=True, vmem_limit_bytes=megabytes * 2**20
        ),
        name=name,
    )(*args)


MESH = pl.DeviceIdType.MESH


def is_far(i):
    return lax.rem(i, 4) == 2


class Plan:
    def __init__(self, feed_rows, mixer_rows, rows):
        self.rows = rows
        self.feed, self.mixer = feed_rows // rows, mixer_rows // 2 // rows
        self.pieces = self.feed + self.mixer + 1
        self.total = self.pieces * rows
        self.feed_rows, self.mixer_rows = feed_rows, mixer_rows


def sum_kernel(
    length, plan, lag,
    up_half_ref, down_half_ref, normed_ref, middle_grad_ref, gated_ref, query_grad_ref, key_grad_ref, value_grad_ref,
    normed_x_ref, narrow_x_ref, wide_y_ref, narrow_y_ref, small_ref, tokens_ref, gain_ref,
    query_hbm, key_hbm, value_hbm,
    out_ref, input_grad_ref,
    sum_ref, got_ref, feed_got_ref, keep_ref, send_ref, mixer_got_ref, small_got_ref, small_sum_ref, weights_ref, local_ref,
    other_ref,
    load_sem, store_sem, chain_send, chain_recv, z_send, z_recv, side_send, side_recv, feed_send, feed_recv,
    mixer_send, mixer_recv, small_send, small_recv, core_send, core_recv
):
    me = lax.axis_index("seq")
    core = lax.axis_index("tp")
    place, quarter = me // 4, lax.rem(me, 4)
    x, y = lax.rem(quarter, 2), quarter // 2
    x_peer, y_peer = me + 1 - 2 * x, me + 2 - 4 * y
    quarter_x, quarter_y, quarter_d = quarter + 1 - 2 * x, quarter + 2 - 4 * y, 3 - quarter
    rows, pieces = plan.rows, plan.pieces
    width = gated_ref.shape[1]
    first = lag * (length - 1)
    started = (place, length - 1 - place)
    ahead = (me + 4, me - 4)
    behind = (me - 4, me + 4)
    side_peers = (x_peer, y_peer)
    side_bits = (x, y)
    halves = (up_half_ref, down_half_ref)
    loads = [
        pltpu.make_async_copy(source, weights_ref.at[n], load_sem.at[n])
        for n, source in enumerate((query_hbm, key_hbm, value_hbm))
    ]
    for load in loads:
        load.start()
    barrier = pltpu.get_barrier_semaphore()

    def greet(peer):
        pl.semaphore_signal(barrier, inc=1, device_id={"seq": peer}, device_id_type=MESH)

    greet(x_peer)
    greet(y_peer)
    pl.semaphore_signal(barrier, inc=1, device_id={"tp": 1 - core}, device_id_type=MESH)
    pl.when(place > 0)(lambda: greet(me - 4))
    pl.when(place < length - 1)(lambda: greet(me + 4))
    pl.semaphore_wait(barrier, 3 + (place > 0).astype(jnp.int32) + (place < length - 1).astype(jnp.int32))

    def remote(source, target, send, recv, peer):
        return pltpu.make_async_remote_copy(
            src_ref=source,
            dst_ref=target,
            send_sem=send,
            recv_sem=recv,
            device_id={"seq": peer},
            device_id_type=MESH,
        )

    def at(i):
        return pl.ds(pl.multiple_of(i * rows, 8), rows)

    def feed_copy(d, i):
        source = pl.ds(pl.multiple_of((1 - side_bits[d]) * plan.feed_rows + i * rows, 8), rows)
        return remote(
            halves[d].at[source], feed_got_ref.at[d, at(i)], feed_send.at[d, i], feed_recv.at[d, i], side_peers[d]
        )

    def send_feed(i, _):
        for d in range(2):
            feed_copy(d, i).start()
        return 0

    lax.fori_loop(0, plan.feed, send_feed, 0)

    def features(ref, h):
        return ref[:, pl.ds(pl.multiple_of(h * width, LANES), width)]

    def query_or_key(h):
        narrow = jnp.where(x == 0, query_grad_ref[...], key_grad_ref[...])
        return dot(features(normed_ref, h), narrow, 0, 0) + dot(features(normed_x_ref, h), narrow_x_ref[...], 0, 0)

    def value_or_out(h):
        left = jnp.where(y == 0, features(normed_ref, h), gated_ref[...])
        right = jnp.where(y == 0, value_grad_ref[...], features(middle_grad_ref, h))
        wide, narrow = features(wide_y_ref, h), narrow_y_ref[...]
        return dot(left, right, 0, 0) + dot(jnp.where(y == 0, wide, narrow), jnp.where(y == 0, narrow, wide), 0, 0)

    mixer_copies = [
        remote(send_ref.at[n], mixer_got_ref.at[n], mixer_send.at[n], mixer_recv.at[n], peer)
        for n, peer in enumerate((y_peer, x_peer))
    ]
    send_ref[0] = query_or_key(1 - y)
    mixer_copies[0].start()
    send_ref[1] = value_or_out(1 - x)
    mixer_copies[1].start()

    def chain_copy(d, i):
        return remote(
            sum_ref.at[d, at(i)], got_ref.at[d, at(i)], chain_send.at[d, i], chain_recv.at[d, i], ahead[d]
        )

    def z_copy(d, i, k):
        ref = out_ref.at[(quarter, quarter_x, quarter_y, quarter_d)[k], d, at(i)]
        return remote(ref, ref, z_send.at[d, i, k], z_recv.at[d, i, k], behind[d])

    def side_copy(d, i, k):
        even = lax.rem(i, 2) == 0
        source = (quarter, quarter, jnp.where(even, quarter_x, quarter_y))[k]
        peer = (x_peer, y_peer, jnp.where(even, y_peer, x_peer))[k]
        ref = out_ref.at[source, d, at(i)]
        return remote(ref, ref, side_send.at[d, i, k], side_recv.at[d, i, k], peer)

    def chain_step(d, i):
        @pl.when(i < plan.feed)
        def _():
            feed_copy(d, i).wait_recv()
            mine = pl.ds(pl.multiple_of(side_bits[d] * plan.feed_rows + i * rows, 8), rows)
            sum_ref[d, at(i)] = halves[d][mine, :] + feed_got_ref[d, at(i)]

        @pl.when(started[d] > 0)
        def _():
            chain_copy(d, i).wait_recv()
            sum_ref[d, at(i)] = sum_ref[d, at(i)] + got_ref[d, at(i)]

        @pl.when(started[d] < length - 1)
        def _():
            chain_copy(d, i).start()

        @pl.when(started[d] == length - 1)
        def _():
            store = pltpu.make_async_copy(sum_ref.at[d, at(i)], out_ref.at[quarter, d, at(i)], store_sem.at[d, i])
            store.start()
            store.wait()

    def kind(d, i):
        remaining = length - 1 - started[d]
        far = is_far(i)
        sideways = jnp.logical_or(jnp.logical_not(far), remaining == 0)
        onward = jnp.logical_and(far, remaining < length - 1)
        return remaining, sideways, onward

    def own_step(d, i):
        remaining, sideways, _ = kind(d, i)

        @pl.when(remaining > 0)
        def _():
            z_copy(d, i, 0).wait_recv()

        @pl.when(remaining < length - 1)
        def _():
            z_copy(d, i, 0).start()

        @pl.when(sideways)
        def _():
            side_copy(d, i, 0).start()
            side_copy(d, i, 1).start()

    def side_step(d, i):
        _, sideways, onward = kind(d, i)

        @pl.when(sideways)
        def _():
            side_copy(d, i, 0).wait_recv()
            side_copy(d, i, 1).wait_recv()
            side_copy(d, i, 2).start()

        @pl.when(jnp.logical_not(sideways))
        def _():
            z_copy(d, i, 1).wait_recv()
            z_copy(d, i, 2).wait_recv()

        @pl.when(onward)
        def _():
            z_copy(d, i, 1).start()
            z_copy(d, i, 2).start()

    def last_step(d, i):
        _, sideways, onward = kind(d, i)

        @pl.when(sideways)
        def _():
            side_copy(d, i, 2).wait_recv()

        @pl.when(jnp.logical_not(sideways))
        def _():
            z_copy(d, i, 3).wait_recv()

        @pl.when(onward)
        def _():
            z_copy(d, i, 3).start()

    def tick(t, _):
        for step, late in ((last_step, first + 2 * lag), (side_step, first + lag), (chain_step, 0), (own_step, first)):
            for d in range(2):
                passed = started[d] if step is chain_step else length - 1 - started[d]
                i = t - late - lag * passed
                pl.when(jnp.logical_and(i >= 0, i < pieces))(functools.partial(step, d, i))
        return 0

    core_copy = pltpu.make_async_remote_copy(
        src_ref=local_ref,
        dst_ref=other_ref,
        send_sem=core_send.at[0],
        recv_sem=core_recv.at[0],
        device_id={"tp": 1 - core},
        device_id_type=MESH,
    )
    small_x = remote(
        small_sum_ref.at[1 - x], small_got_ref.at[pl.ds(0, 2)], small_send.at[0], small_recv.at[0], x_peer
    )
    small_y = remote(
        small_sum_ref.at[x, 1 - y], small_got_ref.at[2], small_send.at[1], small_recv.at[1], y_peer
    )

    def normed_grad():
        for load in loads:
            load.wait()
        local_ref[...] = (
            dot(query_grad_ref[...], weights_ref[0], 1, 1)
            + dot(key_grad_ref[...], weights_ref[1], 1, 1)
            + dot(value_grad_ref[...], weights_ref[2], 1, 1)
        )
        core_copy.start()

    def first_norm():
        core_copy.wait_recv()
        grad = local_ref[...] + other_ref[...]
        values = tokens_ref[...]
        centered = values - over_features(values)
        inverse = lax.rsqrt(over_features(centered * centered) + EPSILON)
        scaled = centered * inverse
        scaled_grad = grad * gain_ref[...]
        scaled_grad = scaled_grad - over_features(scaled_grad) - scaled * over_features(scaled_grad * scaled)
        input_grad_ref[...] = middle_grad_ref[...] + inverse * scaled_grad
        for p in range(4):
            small_sum_ref[p // 2, p % 2] = small_ref[p]
        small_sum_ref[0, 0, pl.ds(STATE // 4, 1), :] = over_tokens(grad * scaled)
        small_sum_ref[0, 0, pl.ds(STATE // 4 + 1, 1), :] = over_tokens(grad)
        small_x.start()

    def keep_mixer():
        keep_ref[0] = query_or_key(y)
        keep_ref[1] = value_or_out(x)

    def add_small():
        small_x.wait()
        small_sum_ref[x] = small_sum_ref[x] + small_got_ref[pl.ds(0, 2)]
        small_y.start()

    def mixer_sums():
        for copy in mixer_copies:
            copy.wait_recv()
        count = plan.mixer_rows // 2
        for d in range(2):
            source, target = pl.ds(d * count, count), pl.ds(plan.feed_rows, count)
            for n in range(2):
                sum_ref[d, target, pl.ds(n * width, width)] = keep_ref[n, source, :] + mixer_got_ref[n, source, :]

    def small_sums():
        small_y.wait()
        last = pl.ds(plan.total - rows, rows)
        sum_ref[0, last, :] = small_sum_ref[x, y] + small_got_ref[2]
        sum_ref[1, last, :] = jnp.zeros_like(sum_ref[1, last, :])

    stages = (
        (2, (normed_grad,)),
        (5, (first_norm,)),
        (8, (keep_mixer, add_small)),
        (plan.feed, (mixer_sums, small_sums)),
    )
    at_tick = 0
    for until, work in stages:
        lax.fori_loop(at_tick, until, tick, 0)
        at_tick = until
        for piece in work:
            piece()
    lax.fori_loop(at_tick, 2 * first + 2 * lag + pieces, tick, 0)

    def drain(i, _):
        for d in range(2):
            remaining, sideways, onward = kind(d, i)
            pl.when(i < plan.feed)(lambda: feed_copy(d, i).wait_send())
            pl.when(remaining > 0)(lambda: chain_copy(d, i).wait_send())
            pl.when(remaining < length - 1)(lambda: z_copy(d, i, 0).wait_send())

            @pl.when(onward)
            def _():
                for k in range(1, 4):
                    z_copy(d, i, k).wait_send()

            @pl.when(sideways)
            def _():
                for k in range(3):
                    side_copy(d, i, k).wait_send()

        return 0

    lax.fori_loop(0, pieces, drain, 0)
    for copy in mixer_copies + [core_copy]:
        copy.wait_send()


def summed_quarters(plan, lag, args, in_hbm, collective_id):
    length = lax.axis_size("seq") // 4
    pieces, feed = plan.pieces, plan.feed
    tokens, columns = args[2].shape
    width = args[4].shape[1]
    sems = [(3,), (2, pieces), (2, pieces), (2, pieces), (2, pieces, 4), (2, pieces, 4), (2, pieces, 3), (2, pieces, 3)]
    sems += [(2, feed), (2, feed), (2,), (2,), (2,), (2,), (1,), (1,)]
    scratch = [(2, plan.total, columns)] * 2 + [(2, plan.feed_rows, columns)] + [(2, plan.mixer_rows, width)] * 3
    scratch += [(3, plan.rows, columns), (2, 2, plan.rows, columns), (3, columns, width)] + [(tokens, columns)] * 2
    return pl.pallas_call(
        functools.partial(sum_kernel, length, plan, lag),
        out_shape=[shape(4, 2, plan.total, columns), shape(tokens, columns)],
        in_specs=[pl.BlockSpec(memory_space=pltpu.HBM if n in in_hbm else pltpu.VMEM) for n in range(len(args))],
        out_specs=[pl.BlockSpec(memory_space=pltpu.HBM), pl.BlockSpec(memory_space=pltpu.VMEM)],
        scratch_shapes=[pltpu.VMEM(dims, F32) for dims in scratch] + [pltpu.SemaphoreType.DMA(dims) for dims in sems],
        compiler_params=pltpu.CompilerParams(
            collective_id=collective_id, has_side_effects=True, vmem_limit_bytes=60 * 2**20
        ),
        name="gradient_sums",
    )(*args)


def unpack_kernel(plan, sums_ref, *refs):
    (
        up_ref, down_ref, query_ref, key_ref, value_ref, out_ref, rate_ref, state_out_ref, wide_ref, narrow_ref, small_ref, sem
    ) = refs
    columns, width = up_ref.shape[0], query_ref.shape[1]
    feed, count, state = plan.feed_rows, plan.mixer_rows // 2, STATE // 4
    copies = []

    def copy(source, target):
        copies.append(pltpu.make_async_copy(source, target, sem.at[len(copies)]))
        copies[-1].start()

    def span(start, size):
        return pl.ds(start, size)

    for x in range(2):
        for y in range(2):
            part = sums_ref.at[2 * y + x]
            copy(part.at[0, span(plan.total - plan.rows, plan.rows)], small_ref.at[2 * x + y])
    for x in range(2):
        for y in range(2):
            part = sums_ref.at[2 * y + x]
            copy(part.at[0, span(0, feed)], up_ref.at[span(x * feed, feed), span(y * columns, columns)])
            copy(part.at[1, span(0, feed)], down_ref.at[span((2 * x + y) * feed, feed)])
            for d in range(2):
                mixer = part.at[d, span(feed, count)]
                target = (query_ref, key_ref)[x]
                copy(mixer.at[:, span(0, width)], target.at[span((2 * y + d) * count, count)])
                if y == 0:
                    target = value_ref.at[span((2 * x + d) * count, count)]
                else:
                    target = out_ref.at[span(d * count, count), span(x * width, width)]
                copy(mixer.at[:, span(width, width)], target)
            rows = span((2 * x + y) * state, state)
            last = part.at[0, span(plan.total - plan.rows, state)]
            copy(last.at[:, span(0, width)], rate_ref.at[rows])
            copy(last.at[:, span(width, width)], state_out_ref.at[rows])
    for n in range(4):
        copies[n].wait()
    wide_ref[...] = small_ref[0, pl.ds(state, 8), :]
    narrow_ref[...] = small_ref[1, pl.ds(state, 8), :]
    for item in copies[4:]:
        item.wait()


def unpacked(plan, sums, outs):
    columns = sums.shape[-1]
    outs = outs + [shape(8, columns)] * 2
    return pl.pallas_call(
        functools.partial(unpack_kernel, plan),
        out_shape=outs,
        in_specs=[pl.BlockSpec(memory_space=pl.ANY)],
        out_specs=[pl.BlockSpec(memory_space=pltpu.HBM)] * (len(outs) - 2) + [pl.BlockSpec(memory_space=pltpu.VMEM)] * 2,
        scratch_shapes=[pltpu.VMEM((4, plan.rows, columns), F32), pltpu.SemaphoreType.DMA((64,))],
        compiler_params=pltpu.CompilerParams(vmem_limit_bytes=16 * 2**20),
        name="unpack",
    )(sums)


def matmul(left, right):
    return jnp.dot(left, right, precision=PRECISION, preferred_element_type=F32)


def layer_norm(values, gain, bias):
    centered = values - jnp.mean(values, axis=-1, keepdims=True)
    spread = jnp.mean(centered * centered, axis=-1, keepdims=True)
    return centered * lax.rsqrt(spread + EPSILON) * gain + bias


def decay_terms(log_step, state_rate):
    decay_rate = jnp.exp(log_step)[None, :] * state_rate
    return (jnp.exp(-decay_rate), jnp.sqrt(-jnp.expm1(-2.0 * decay_rate)))


def on_device(
    tokens,
    cotangent,
    norm1_gain,
    norm1_bias,
    query_weight,
    query_bias,
    key_weight,
    key_bias,
    value_weight,
    value_bias,
    shift_kernel,
    log_step,
    state_rate,
    state_out,
    skip_gain,
    out_weight,
    out_bias,
    norm2_gain,
    norm2_bias,
    up_weight,
    up_bias,
    down_weight,
    down_bias,
):
    tok_rows = tokens.shape[0]
    width_local = query_weight.shape[1]
    span = lax.axis_size("seq") // SEQS
    chunks = tok_rows // CHUNK
    normed = layer_norm(tokens, norm1_gain, norm1_bias)
    queries = matmul(normed, query_weight) + query_bias
    key_rows = matmul(normed, key_weight) + key_bias
    value_rows = matmul(normed, value_weight) + value_bias
    decay_rate = jnp.exp(log_step)[None, :] * state_rate
    decay_factor, in_coef = decay_terms(log_step, state_rate)
    device_decay = jnp.exp(-decay_rate * tok_rows)
    out_coef = in_coef * state_out
    skip_row = skip_gain[None, :]
    tok_shape, state_shape = shape(tok_rows, width_local), shape(STATE, width_local)
    gated, ssm_out, mixed, shifted, starts, halo = mixer_call(
        mixer_kernel,
        span,
        (queries, key_rows, value_rows, shift_kernel, skip_row, decay_factor, out_coef, device_decay),
        [tok_shape] * 4 + [shape(chunks, STATE, width_local), shape(8, width_local)],
        [(tok_rows + 8, width_local), (width_local // LANES, tok_rows, LANES), (CHUNK, 8, LANES)],
        width_local,
        1,
        "mixer",
    )
    hidden, columns = up_weight.shape[1], tokens.shape[1]
    plan = Plan(columns // 2, width_local, PIECE_ROWS)
    wide_shape = shape(*tokens.shape)
    (
        block_out,
        grad_middle,
        grad_queries,
        grad_keys,
        grad_values,
        small,
        down_half,
        up_half,
        normed_x,
        narrow_x,
        wide_y,
        narrow_y,
    ) = mixer_call(
        layer_kernel,
        span,
        (gated, tokens, cotangent, out_weight, out_bias[None], norm2_gain[None], norm2_bias[None], up_weight)
        + (up_bias[None], down_weight, down_bias[None], queries, key_rows, value_rows, halo, ssm_out, mixed, shifted)
        + (starts, shift_kernel, skip_row, decay_factor, out_coef, device_decay)
        + (normed, in_coef, decay_factor * decay_factor / in_coef * state_out, decay_rate, jnp.exp(log_step)[None]),
        [wide_shape] * 2
        + [tok_shape] * 3
        + [shape(4, PIECE_ROWS, columns)]
        + [shape(hidden // 2, columns), shape(columns, hidden // 2)]
        + [wide_shape, tok_shape, wide_shape, tok_shape],
        [up_weight.shape, down_weight.shape, (2, tok_rows, hidden // 2), (2, tok_rows, hidden // 2)]
        + [tokens.shape] * 9
        + [(tok_rows, hidden // 2)] * 2
        + [tokens.shape] * 2
        + [(tok_rows, width_local)] * 2
        + [(width_local // LANES, tok_rows, LANES)] * 2
        + [(tok_rows + 8, width_local), (tok_rows + 8, width_local), (8, width_local)]
        + [(CHUNK, 8, LANES), (CHUNK, STATE, LANES)]
        + [(STATE, width_local)] * 2,
        width_local,
        2,
        "layer",
        [(2,), (4,), (4,), (4,), (4,), (4, 2), (4, 2)],
        (7, 9),
        60,
    )
    sums, input_grad = summed_quarters(
        plan,
        LAG,
        (up_half, down_half, normed, grad_middle, gated, grad_queries, grad_keys, grad_values, normed_x, narrow_x)
        + (wide_y, narrow_y, small, tokens, norm1_gain[None], query_weight, key_weight, value_weight),
        (15, 16, 17),
        3,
    )
    weights = (up_weight, down_weight, query_weight, key_weight, value_weight, out_weight, state_rate, state_out)
    (
        grad_up_weight,
        grad_down_weight,
        grad_query_weight,
        grad_key_weight,
        grad_value_weight,
        grad_out_weight,
        grad_state_rate,
        grad_state_out,
        wide,
        narrow,
    ) = unpacked(plan, sums, [shape(*weight.shape) for weight in weights])
    grad_norm1_gain, grad_norm1_bias, grad_norm2_gain, grad_norm2_bias, grad_out_bias, grad_down_bias = (
        wide[k] for k in range(6)
    )
    grad_up_bias = wide[6:8].reshape(-1)
    narrow = narrow.reshape(-1, width_local)
    grad_skip_gain, grad_shift_kernel, grad_log_step = narrow[0], narrow[1:5], narrow[8]
    grad_query_bias, grad_key_bias, grad_value_bias = narrow[5], narrow[6], narrow[7]
    return (
        block_out,
        input_grad,
        grad_norm1_gain,
        grad_norm1_bias,
        grad_query_weight,
        grad_query_bias,
        grad_key_weight,
        grad_key_bias,
        grad_value_weight,
        grad_value_bias,
        grad_shift_kernel,
        grad_log_step,
        grad_state_rate,
        grad_state_out,
        grad_skip_gain,
        grad_out_weight,
        grad_out_bias,
        grad_norm2_gain,
        grad_norm2_bias,
        grad_up_weight,
        grad_up_bias,
        grad_down_weight,
        grad_down_bias,
    )


def solution(mesh):
    return jax.shard_map(
        on_device,
        mesh=mesh,
        in_specs=(
            P("seq", None),
            P("seq", None),
            P(),
            P(),
            P(None, "tp"),
            P("tp"),
            P(None, "tp"),
            P("tp"),
            P(None, "tp"),
            P("tp"),
            P(None, "tp"),
            P("tp"),
            P(None, "tp"),
            P(None, "tp"),
            P("tp"),
            P("tp", None),
            P(),
            P(),
            P(),
            P(None, "tp"),
            P("tp"),
            P("tp", None),
            P(),
        ),
        out_specs=(
            P("seq", None),
            P("seq", None),
            P(),
            P(),
            P(None, "tp"),
            P("tp"),
            P(None, "tp"),
            P("tp"),
            P(None, "tp"),
            P("tp"),
            P(None, "tp"),
            P("tp"),
            P(None, "tp"),
            P(None, "tp"),
            P("tp"),
            P("tp", None),
            P(),
            P(),
            P(),
            P(None, "tp"),
            P("tp"),
            P("tp", None),
            P(),
        ),
        check_vma=False,
    )
```

profile of v0, /device:TPU:0, one launch (start us, length us, event | category | flops | bytes accessed | tf_op | source)
XLA Modules:
  0.0 296.3 jit_solution(8227663135330884360)
XLA Ops:
  0.8 1.4 reduce_sum.18
  6.6 0.7 divide_multiply_fusion
  7.3 0.7 negate_sqrt_fusion
  8.7 0.8 convolution_add_fusion.value_ref
  9.5 0.7 copy-done.18
  10.2 0.8 convolution_add_fusion.1.key_ref
  11.6 0.8 convolution_add_fusion.2.query_ref
  12.6 18.6 %mixer.1 = (f32[256,384]{1,0:T(8,128)S(1)}, f32[256,384]{1,0:T(8,128)S(1)}, f32[256,384]{1,0:T(8,128)S(1)}, f32[256,384]{1,0:T(8,128)S(1)}, f32[8,64,384]{2,1,0:T(8,128)S(1)}, /*index=5*/f32[8,384]{1,0:T(8,128)S(1)}) custom-call(f32[256,384]{1,0:T(8,128)S(1)} %convolution_add_fusion.2.query_ref, f32[256,384]{1,0:T(8,128)S(1)} %convolution_add_fusion.1.key_ref, ...), custom_call_target="tpu_custom_call" | custom-call | tf_op jit(solution)/shard_map/mixer/pallas_call | solution.py:523
  31.2 0.7 copy-done.4
  32.0 0.9 copy-done.8
  32.8 0.7 copy-done.9
  33.6 0.7 copy-done.10
  34.3 0.7 copy-done.11
  35.1 0.6 copy-done.14
  35.7 68.7 %layer.1 = (f32[256,768]{1,0:T(8,128)}, f32[256,768]{1,0:T(8,128)}, f32[256,384]{1,0:T(8,128)}, f32[256,384]{1,0:T(8,128)}, f32[256,384]{1,0:T(8,128)}, /*index=...) custom-call(f32[256,384]{1,0:T(8,128)} %copy-done.4, ...), custom_call_target="tpu_custom_call" | custom-call | tf_op jit(solution)/shard_map/layer/pallas_call | solution.py:523
  104.4 176.5 %gradient_sums.1 = (f32[4,2,600,768]{3,2,1,0:T(8,128)}, f32[256,768]{1,0:T(8,128)}) custom-call(f32[768,768]{1,0:T(8,128)} %get-tuple-element.60.up_half_ref, f32[768,768]{1,0:T(8,128)} %get-tuple-element.61.down_half_ref, f32[256,768]{1,0:T(8,128)} %copy-done.15, f32[256,768]{1,0:T(8,128)} %get-tuple-element.62.middle_grad_ref, f32[256,384]{1,0:T(8,128)} %copy-done.4, ...), custom_call_target="tpu_custom_call" | custom-call | tf_op jit(solution)/shard_map/gradient_sums/pallas_call | solution.py:859
  280.9 5.2 %copy-done = f32[4,2,600,768]{3,2,1,0:T(8,128)S(1)} copy-done((f32[4,2,600,768]{3,2,1,0:T(8,128)S(1)}, f32[4,2,600,768]{3,2,1,0:T(8,128)}, u32[]{:S(2)}) %copy-start) | copy-done | bytes 14745624
  286.1 6.0 %unpack.1 = (f32[768,1536]{1,0:T(8,128)}, f32[1536,768]{1,0:T(8,128)}, f32[768,384]{1,0:T(8,128)}, f32[768,384]{1,0:T(8,128)}, f32[768,384]{1,0:T(8,128)}, /*ind...) custom-call(f32[4,2,600,768]{3,2,1,0:T(8,128)S(1)} %copy-done), custom_call_target="tpu_custom_call" | custom-call | tf_op jit(solution)/shard_map/unpack/pallas_call | solution.py:920
  292.1 0.6 slice_reduce_fusion
  292.7 0.6 reshape.71
  293.4 0.6 slice.55
  294.0 0.6 slice_reduce_fusion.6
  294.6 0.9 copy.48
  295.5 0.9 copy.49
  (81 shorter events, 5.6 us)
Async XLA Ops:
  0.7 5.9 %copy-start.23 = (f32[64,384]{1,0:T(8,128)S(1)}, f32[64,384]{1,0:T(8,128)}, u32[]{:S(2)}) copy-start(f32[64,384]{1,0:T(8,128)} %param.36) | copy-start | bytes 294916
  0.7 4.7 %copy-start.25 = (f32[768]{0:T(1024)S(1)}, f32[768]{0:T(1024)}, u32[]{:S(2)}) copy-start(f32[768]{0:T(1024)} %param.25) | copy-start | bytes 9220
  0.7 4.1 %copy-start.31 = (f32[768]{0:T(1024)S(1)}, f32[768]{0:T(1024)}, u32[]{:S(2)}) copy-start(f32[768]{0:T(1024)} %param.45) | copy-start | bytes 9220
  0.7 5.3 %copy-start.26 = (f32[1536]{0:T(1024)S(1)}, f32[1536]{0:T(1024)}, u32[]{:S(2)}) copy-start(f32[1536]{0:T(1024)} %param.43) | copy-start | bytes 18436
  0.7 3.5 %copy-start.30 = (f32[768]{0:T(1024)S(1)}, f32[768]{0:T(1024)}, u32[]{:S(2)}) copy-start(f32[768]{0:T(1024)} %param.41) | copy-start | bytes 9220
  0.7 2.9 copy-start.29
  0.7 2.3 copy-start.28
  0.7 1.7 copy-start.32
  0.8 5.8 %copy-start.24 = (f32[64,384]{1,0:T(8,128)S(1)}, f32[64,384]{1,0:T(8,128)}, u32[]{:S(2)}) copy-start(f32[64,384]{1,0:T(8,128)} %param.35) | copy-start | bytes 294916
  0.8 1.7 copy-start.33
  0.8 7.3 %copy-start.27 = (f32[768]{0:T(1024)S(1)}, f32[768]{0:T(1024)}, u32[]{:S(2)}) copy-start(f32[768]{0:T(1024)} %param.26) | copy-start | bytes 9220
  2.5 10.0 %copy-start.13 = (f32[1,384]{1,0:T(1,128)}, f32[1,384]{1,0:T(1,128)S(1)}, u32[]{:S(2)}) copy-start(f32[1,384]{1,0:T(1,128)S(1)} %broadcast_in_dim.16.skip_ref) | copy-start | bytes 4612
  7.3 2.2 copy-start.20
  8.1 4.5 %copy-start.5 = (f32[64,384]{1,0:T(8,128)}, f32[64,384]{1,0:T(8,128)S(1)}, u32[]{:S(2)}) copy-start(f32[64,384]{1,0:T(8,128)S(1)} %get-tuple-element.97.out_coef_ref) | copy-start | bytes 294916
  8.1 4.5 %copy-start.6 = (f32[64,384]{1,0:T(8,128)}, f32[64,384]{1,0:T(8,128)S(1)}, u32[]{:S(2)}) copy-start(f32[64,384]{1,0:T(8,128)S(1)} %get-tuple-element.98.device_decay_ref) | copy-start | bytes 294916
  8.1 4.5 %copy-start.7 = (f32[64,384]{1,0:T(8,128)}, f32[64,384]{1,0:T(8,128)S(1)}, u32[]{:S(2)}) copy-start(f32[64,384]{1,0:T(8,128)S(1)} %get-tuple-element.99.decay_ref) | copy-start | bytes 294916
  8.7 2.4 copy-start.15
  8.7 1.6 copy-start.18
  8.7 1.6 copy-start.35
  10.2 2.3 copy-start.1
  12.6 23.1 %copy-start.3 = (f32[256,384]{1,0:T(8,128)}, f32[256,384]{1,0:T(8,128)S(1)}, u32[]{:S(2)}) copy-start(f32[256,384]{1,0:T(8,128)S(1)} %convolution_add_fusion.2.query_ref) | copy-start | bytes 1179652
  280.9 5.2 %copy-start = (f32[4,2,600,768]{3,2,1,0:T(8,128)S(1)}, f32[4,2,600,768]{3,2,1,0:T(8,128)}, u32[]{:S(2)}) copy-start(f32[4,2,600,768]{3,2,1,0:T(8,128)} %get-tuple-element.72.sums_ref) | copy-start | bytes 44236804
  286.1 8.5 %copy-start.21 = (f32[256,768]{1,0:T(8,128)S(1)}, f32[256,768]{1,0:T(8,128)}, u32[]{:S(2)}) copy-start(f32[256,768]{1,0:T(8,128)} %get-tuple-element.123) | copy-start | bytes 2359300
  292.1 3.4 %copy-start.22 = (f32[256,768]{1,0:T(8,128)S(1)}, f32[256,768]{1,0:T(8,128)}, u32[]{:S(2)}) copy-start(f32[256,768]{1,0:T(8,128)} %get-tuple-element.124) | copy-start | bytes 2359300
  (13 other events, 13.3 us)
where the time goes:
time: 297 us; the launch traced here: 296 us
  Pallas kernels  270 us (91%)
  local copies, waits for them, and re-layouts  19.7 us (7%)
  other arithmetic  3.3 us (1%)
    pallas_call x1, Pallas kernels, summed_quarters(): pl.pallas_call(functools.partial(sum_kernel, length, plan, lag), out_shap...  176 us
    pallas_call x2, Pallas kernels, mixer_call(): pl.pallas_call(functools.partial(kernel, span), in_specs=[pl.BlockSpec(me...  87.3 us
    unnamed x76, local copies, waits for them, and re-layouts  13.2 us
    pallas_call x1, Pallas kernels, unpacked(): pl.pallas_call(functools.partial(unpack_kernel, plan), out_shape=outs, in...  5.99 us

commit v1 on v0

v1 whole, which is shorter than its diff:
```python
import functools
import types

import jax
import jax.numpy as jnp
from jax import lax
from jax.experimental import pallas as pl
from jax.experimental.pallas import tpu as pltpu
from jax.sharding import PartitionSpec as P

SHIFT = 4
SEQS = 2
STATE = 64
LANES = 128
CHUNK = 32
PIECE_ROWS = 24
LAG = 2
SPREAD = 3
WINDOW = 3
GELU_SCALE = (2.0 / 3.141592653589793) ** 0.5

EPSILON = 1e-05
F32 = jnp.float32
PRECISION = lax.Precision.HIGH


def shape(*dims):
    return jax.ShapeDtypeStruct(dims, F32)


def fold_states(values):
    return jnp.sum(values.reshape(STATE // 8, 8, LANES), axis=0)


def cut(block):
    return pl.ds(block * LANES, LANES)


class Sequence:
    def __init__(self, span, backward):
        self.me = lax.axis_index("seq")
        self.span = span
        self.place = lax.rem(self.me, span)
        self.start = self.me - self.place
        self.groups = span // 4
        self.quarter, self.group = lax.rem(self.place, 4), self.place // 4
        if backward:
            self.rank, self.turn = 3 - self.quarter, self.groups - 1 - self.group
        else:
            self.rank, self.turn = self.quarter, self.group
        self.backward = backward

    def greet(self, other_core):
        barrier = pltpu.get_barrier_semaphore()
        for k in range(1, self.span):
            peer = self.start + lax.rem(self.place + k, self.span)
            pl.semaphore_signal(barrier, inc=1, device_id={"seq": peer}, device_id_type=pl.DeviceIdType.MESH)
        pl.semaphore_signal(barrier, inc=1, device_id={"tp": other_core}, device_id_type=pl.DeviceIdType.MESH)

    def greeted(self):
        pl.semaphore_wait(pltpu.get_barrier_semaphore(), self.span)

    def remote(self, source, target, send, recv, peer, core=None):
        return pltpu.make_async_remote_copy(
            src_ref=source,
            dst_ref=target,
            send_sem=send,
            recv_sem=recv,
            device_id={"seq": peer} if core is None else {"tp": core},
            device_id_type=pl.DeviceIdType.MESH,
        )

    def end_copy(self, b, k, ends_ref, sems):
        other = lax.rem(self.quarter + k, 4)
        peer = self.me - self.quarter + other
        ref = ends_ref.at[self.rank, :, cut(b)]
        return self.remote(ref, ref, sems[0].at[b, k - 1], sems[1].at[b, k - 1], peer)

    def total_copy(self, b, k, totals_ref, sems):
        peer = self.me - 4 * k if self.backward else self.me + 4 * k
        ref = totals_ref.at[self.turn, :, cut(b)]
        return self.remote(ref, ref, sems[2].at[b, k - 1], sems[3].at[b, k - 1], peer)

    def send_end(self, b, end, ends_ref, sems):
        ends_ref[self.rank, :, cut(b)] = end
        for k in range(1, 4):
            self.end_copy(b, k, ends_ref, sems).start()

    def group_total(self, b, decay, ends_ref, totals_ref, sems):
        for k in range(1, 4):
            self.end_copy(b, k, ends_ref, sems).wait_recv()
        before = jnp.zeros_like(decay)
        total = ends_ref[0, :, cut(b)]
        for r in range(3):
            before = jnp.where(self.rank > r, before * decay + ends_ref[r, :, cut(b)], before)
            total = total * decay + ends_ref[r + 1, :, cut(b)]
        if self.groups > 1:
            totals_ref[self.turn, :, cut(b)] = total
            for k in range(1, self.groups):
                pl.when(self.turn + k < self.groups)(lambda: self.total_copy(b, k, totals_ref, sems).start())
        return before

    def carried(self, b, decay, before, totals_ref, sems):
        if self.groups == 1:
            return before
        square = decay * decay
        fourth = square * square
        carry = jnp.zeros_like(decay)
        for h in range(self.groups - 1):
            for k in range(1, self.groups - h):
                pl.when(self.turn == h + k)(lambda: self.total_copy(b, k, totals_ref, sems).wait_recv())
        for h in range(self.groups - 1):
            carry = jnp.where(self.turn > h, carry * fourth + totals_ref[h, :, cut(b)], carry)
        for r in range(3):
            carry = jnp.where(self.rank > r, carry * decay, carry)
        return before + carry

    def drain(self, blocks, ends_ref, totals_ref, sems):
        for b in range(blocks):
            for k in range(1, 4):
                self.end_copy(b, k, ends_ref, sems).wait_send()
            for k in range(1, self.groups):
                pl.when(self.turn + k < self.groups)(lambda: self.total_copy(b, k, totals_ref, sems).wait_send())


def dot(left, right, left_axis, right_axis):
    return lax.dot_general(
        left, right, (((left_axis,), (right_axis,)), ((), ())), precision=PRECISION, preferred_element_type=F32
    )


def over_tokens(values):
    return jnp.sum(values, axis=0, keepdims=True)


def over_features(values):
    return jnp.mean(values, axis=1, keepdims=True)


class Share:
    def __init__(self, seq, source_ref, target_ref, send, recv, peer, core, other_core):
        self.source_ref, self.target_ref, self.send, self.recv = source_ref, target_ref, send, recv
        self.seq, self.peer, self.core, self.other_core = seq, peer, core, other_core
        size = source_ref.shape[0] // 2
        self.mine = pl.ds(pl.multiple_of(core * size, 8), size)

    def across(self):
        return self.seq.remote(
            self.source_ref.at[self.mine], self.target_ref.at[self.mine], self.send.at[0], self.recv.at[0], self.peer
        )

    def between(self):
        ref = self.target_ref.at[self.mine]
        return self.seq.remote(ref, ref, self.send.at[1], self.recv.at[1], self.seq.me, self.other_core)

    def relay(self):
        self.across().wait_recv()
        self.between().start()

    def finish(self):
        self.between().wait_recv()
        self.across().wait_send()
        self.between().wait_send()


def one_less_exp(values):
    series = jnp.ones_like(values)
    for k in range(8, 1, -1):
        series = 1.0 - values * series * (1.0 / k)
    return jnp.where(values < 0.25, values * series, 1.0 - jnp.exp(-values))


def front_kernel(names, span, *refs):
    r = types.SimpleNamespace(**dict(zip(names, refs)))
    tokens, width = r.gated.shape
    hidden_half = r.up.shape[1] // 2
    blocks, chunks, top = width // LANES, tokens // CHUNK, tokens // 2
    ahead, back = Sequence(span, False), Sequence(span, True)
    ahead_sems = (r.end_send, r.end_recv, r.total_send, r.total_recv)
    back_sems = (r.back_end_send, r.back_end_recv, r.back_total_send, r.back_total_recv)
    me, remote = ahead.me, ahead.remote
    x, y = lax.rem(me, 2), lax.rem(me // 2, 2)
    x_peer, y_peer = me + 1 - 2 * x, me + 2 - 4 * y
    core = lax.axis_index("tp")
    other_core = 1 - core
    first, last = ahead.place == 0, ahead.place == span - 1

    pairs = (
        (r.tokens_hbm, r.tokens),
        (r.key_hbm, r.key_weight),
        (r.value_hbm, r.value_weight),
        (r.query_hbm, r.query_weight),
        (r.cotangent_hbm, r.cotangent),
        (r.down_hbm, r.down),
        (r.out_hbm, r.out_weight),
        (r.up_hbm, r.up),
    )
    loads = [pltpu.make_async_copy(source, target, r.load_sem.at[n]) for n, (source, target) in enumerate(pairs)]
    for load in loads:
        load.start()
    ahead.greet(other_core)
    vectors = (r.norm1_gain, r.norm1_bias, r.out_bias, r.norm2_gain, r.norm2_bias, r.down_bias)
    for k, vector in enumerate(vectors):
        r.wide[k : k + 1, :] = vector[...].reshape(1, -1)
    for k in range(2):
        r.wide[6 + k : 7 + k, :] = r.up_bias[pl.ds(k * hidden_half, hidden_half)].reshape(1, -1)
    for k, vector in enumerate((r.query_bias, r.key_bias, r.value_bias, r.skip_gain)):
        r.narrow[k : k + 1, :] = vector[...].reshape(1, -1)
    step = jnp.exp(r.log_step[...].reshape(1, -1))
    r.narrow[4:5, :] = step
    r.narrow[5 : 5 + SHIFT, :] = r.taps[...]
    rate = step * r.state_rate[...]
    decay = jnp.exp(-rate)
    in_coef = jnp.sqrt(one_less_exp(2.0 * rate))
    out_coef = in_coef * r.state_out[...]
    r.rate[...] = rate
    r.decay[...] = decay
    r.in_coef[...] = in_coef
    r.out_coef[...] = out_coef
    r.device_decay[...] = jnp.exp(-rate * tokens)
    r.coef_rate[...] = decay * decay / in_coef * r.state_out[...]
    stores = []

    def store(source, target):
        stores.append(pltpu.make_async_copy(source, target, r.store_sem.at[len(stores)]))
        stores[-1].start()

    def wide(k):
        return r.wide[k : k + 1, :]

    def narrow(k):
        return r.narrow[k : k + 1, :]

    def tap(j):
        return narrow(5 + j)

    def features(b):
        return slice(b * LANES, (b + 1) * LANES)

    loads[0].wait()
    values = r.tokens[...]
    centered = values - over_features(values)
    normed = centered * lax.rsqrt(over_features(centered * centered) + EPSILON) * wide(0) + wide(1)
    r.normed1[...] = normed
    store(r.normed1, r.normed1_hbm)
    loads[1].wait()
    r.keys[pl.ds(8, tokens), :] = dot(r.normed1[...], r.key_weight[...], 1, 0) + narrow(1)
    ahead.greeted()

    def halo_copy():
        return remote(
            r.keys.at[pl.ds(tokens, 8)], r.keys.at[pl.ds(0, 8)], r.halo_send.at[0], r.halo_recv.at[0], me + 1
        )

    @pl.when(jnp.logical_not(last))
    def _():
        halo_copy().start()

    loads[2].wait()
    r.value[...] = dot(r.normed1[...], r.value_weight[...], 1, 0) + narrow(2)

    def mix(start, count):
        total = tap(0) * r.keys[pl.ds(8 + start, count), :]
        for j in range(1, SHIFT):
            total = total + tap(j) * r.keys[pl.ds(8 + start - j, count), :]
        r.shifted[pl.ds(start, count), :] = total
        mixed = total * r.value[pl.ds(start, count), :]
        r.mixed[pl.ds(start, count), :] = mixed
        for b in range(blocks):
            r.rows[b, pl.ds(start, count), :] = mixed[:, features(b)]

    mix(8, tokens - 8)

    @pl.when(first)
    def _():
        r.keys[pl.ds(0, 8), :] = jnp.zeros((8, width), F32)

    @pl.when(jnp.logical_not(first))
    def _():
        halo_copy().wait_recv()

    mix(0, 8)

    for b in range(blocks):
        decay, out_coef = r.decay[:, cut(b)], r.out_coef[:, cut(b)]

        def scan(k, state, b=b, decay=decay, out_coef=out_coef):
            r.starts[k, :, cut(b)] = state
            base = pl.multiple_of(k * CHUNK, CHUNK)
            for j in range(CHUNK):
                state = decay * state + r.rows[b, pl.ds(base + j, 1), :]
                r.part[j] = fold_states(out_coef * state)
            r.out[pl.ds(base, CHUNK), cut(b)] = jnp.sum(r.part[...], axis=1)
            return state

        ahead.send_end(b, lax.fori_loop(0, chunks, scan, jnp.zeros_like(decay)), r.ends, ahead_sems)
    loads[3].wait()
    r.query[...] = dot(r.normed1[...], r.query_weight[...], 1, 0) + narrow(0)
    befores = [ahead.group_total(b, r.device_decay[:, cut(b)], r.ends, r.totals, ahead_sems) for b in range(blocks)]
    loads[4].wait()
    loads[5].wait()
    for n in range(2):
        r.pre_grad[n] = dot(r.cotangent[...], r.down[pl.ds(n * hidden_half, hidden_half), :], 1, 1)
    incoming = [
        ahead.carried(b, r.device_decay[:, cut(b)], befores[b], r.totals, ahead_sems) for b in range(blocks)
    ]

    cotangent_share = Share(
        ahead, r.cotangent, r.cotangent_peer, r.share_send.at[0], r.share_recv.at[0], x_peer, core, other_core
    )
    normed2_share = Share(
        ahead, r.normed2, r.normed2_peer, r.share_send.at[1], r.share_recv.at[1], y_peer, core, other_core
    )
    normed1_share = Share(
        ahead, r.normed1, r.normed1_x, r.share_send.at[2], r.share_recv.at[2], x_peer, core, other_core
    )
    wide_shares = [
        Share(ahead, source, r.wide_y, r.share_send.at[3], r.share_recv.at[3], y_peer, core, other_core)
        for source in (r.middle_grad, r.normed1)
    ]

    def narrow_copy(source, n, target, peer):
        return remote(source, target, r.half_send.at[n], r.half_recv.at[n], peer)

    def key_copy():
        return narrow_copy(r.key_grad, 2, r.narrow_x, x_peer)

    def query_copy():
        return narrow_copy(r.query_grad, 2, r.narrow_x, x_peer)

    def gated_copy():
        return narrow_copy(r.gated, 3, r.narrow_y, y_peer)

    def value_copy():
        return narrow_copy(r.value_grad, 3, r.narrow_y, y_peer)

    cotangent_share.across().start()

    @pl.when(y == 1)
    def _():
        wide_shares[1].across().start()

    for b in range(blocks):
        decay, out_coef = r.decay[:, cut(b)], r.out_coef[:, cut(b)]
        skip = narrow(3)[:, features(b)]

        def carry(k, state, b=b, decay=decay, out_coef=out_coef, skip=skip):
            r.starts[k, :, cut(b)] = r.starts[k, :, cut(b)] + state
            base = pl.multiple_of(k * CHUNK, CHUNK)
            for j in range(CHUNK):
                state = decay * state
                r.part[j] = fold_states(out_coef * state)
            rows = pl.ds(base, CHUNK)
            out = r.out[rows, cut(b)] + jnp.sum(r.part[...], axis=1) + skip * r.mixed[rows, cut(b)]
            r.out[rows, cut(b)] = out
            r.gated[rows, cut(b)] = r.query[rows, cut(b)] * out
            return state

        lax.fori_loop(0, chunks, carry, incoming[b])
    store(r.gated, r.gated_hbm)

    def core_copy(n, source, target):
        return remote(source, target, r.core_send.at[n], r.core_recv.at[n], me, other_core)

    loads[6].wait()
    merged_copies = []
    for n in range(2):
        rows = pl.ds(n * top, top)
        r.merged[rows, :] = dot(r.gated[rows, :], r.out_weight[...], 1, 0)
        copy = core_copy(n, r.merged.at[rows], r.merged_other.at[rows])
        copy.start()
        merged_copies.append(copy)

    @pl.when(y == 0)
    def _():
        gated_copy().start()

    normed1_share.across().start()
    small_start = STATE // 4
    r.small[...] = jnp.zeros_like(r.small)

    def put(k, row):
        r.small[1, pl.ds(small_start + k // 2, 1), pl.ds(k % 2 * width, width)] = row

    spreads = []
    for n, copy in enumerate(merged_copies):
        rows = pl.ds(n * top, top)
        copy.wait_recv()
        middle = r.tokens[rows, :] + (r.merged[rows, :] + r.merged_other[rows, :]) + wide(2)
        centered = middle - over_features(middle)
        inverse = lax.rsqrt(over_features(centered * centered) + EPSILON)
        scaled = centered * inverse
        r.middle[rows, :] = middle
        r.scaled[rows, :] = scaled
        r.normed2[rows, :] = scaled * wide(3) + wide(4)
        spreads.append(inverse)
    normed2_share.across().start()

    loads[7].wait()
    for n in range(2):
        part = pl.ds(n * hidden_half, hidden_half)
        pre = dot(r.normed2[...], r.up[:, part], 1, 0) + wide(6 + n)
        square = pre * pre
        curve = jnp.tanh(GELU_SCALE * (pre + 0.044715 * (square * pre)))
        r.active[n] = 0.5 * pre * (1.0 + curve)
        slope = 0.5 * (1.0 + curve) + 0.5 * pre * (1.0 - curve * curve) * (
            GELU_SCALE * (1.0 + 3 * 0.044715 * square)
        )
        pre_grad = r.pre_grad[n] * slope
        r.pre_grad[n] = pre_grad
        r.small[0, pl.ds(small_start + 6 + n, 1), :] = over_tokens(pre_grad)
        normed_grad = dot(pre_grad, r.up[:, part], 1, 1)
        if n == 0:
            r.normed_grad[...] = normed_grad
        else:
            r.normed_grad[...] = r.normed_grad[...] + normed_grad
    normed_grad_copy = core_copy(2, r.normed_grad, r.normed_grad_other)
    normed_grad_copy.start()
    for n in range(2):
        feed = dot(r.active[n], r.down[pl.ds(n * hidden_half, hidden_half), :], 1, 0)
        if n == 0:
            r.feed[...] = feed
        else:
            r.feed[...] = r.feed[...] + feed
    feed_copy = core_copy(3, r.feed, r.feed_other)
    feed_copy.start()
    normed_grad_copy.wait_recv()
    for n in range(2):
        rows = pl.ds(n * top, top)
        normed_grad = r.normed_grad[rows, :] + r.normed_grad_other[rows, :]
        scaled = r.scaled[rows, :]
        scaled_grad = normed_grad * wide(3)
        centered = scaled_grad - over_features(scaled_grad) - scaled * over_features(scaled_grad * scaled)
        middle_grad = r.cotangent[rows, :] + spreads[n] * centered
        r.middle_grad[rows, :] = middle_grad
        sums = (normed_grad * scaled, normed_grad, middle_grad, r.cotangent[rows, :])
        for k, values in enumerate(sums):
            row = pl.ds(small_start + 2 + k, 1)
            if n == 0:
                r.small[0, row, :] = over_tokens(values)
            else:
                r.small[0, row, :] = r.small[0, row, :] + over_tokens(values)
        r.gated_grad[rows, :] = dot(middle_grad, r.out_weight[...], 1, 1)
    store(r.middle_grad, r.middle_grad_hbm)

    grad = r.gated_grad[...] * r.query[...]
    r.grad[...] = grad
    for b in range(blocks):
        r.grad_rows[b] = grad[:, features(b)]
    for b in range(blocks):
        decay = r.decay[:, cut(b)]

        def end(i, adjoint, b=b, decay=decay):
            base = pl.multiple_of((chunks - 1 - i) * CHUNK, CHUNK)
            for j in range(CHUNK - 1, -1, -1):
                adjoint = decay * adjoint + r.grad_rows[b, pl.ds(base + j, 1), :]
            return adjoint

        back.send_end(b, lax.fori_loop(0, chunks, end, jnp.zeros_like(decay)), r.back_ends, back_sems)
    query_grad = r.gated_grad[...] * r.out[...]
    r.query_grad[...] = query_grad
    store(r.query_grad, r.query_grad_hbm)
    put(0, over_tokens(r.grad[...] * r.mixed[...]))
    put(5, over_tokens(query_grad))
    cotangent_share.relay()
    normed1_share.relay()
    normed2_share.relay()
    feed_copy.wait_recv()
    r.block_out[...] = r.middle[...] + (r.feed[...] + r.feed_other[...]) + wide(5)
    store(r.block_out, r.block_out_hbm)
    befores = [
        back.group_total(b, r.device_decay[:, cut(b)], r.back_ends, r.back_totals, back_sems) for b in range(blocks)
    ]

    def product(left_ref, right_ref):
        return dot(left_ref[...], right_ref[...], 0, 0)

    r.down_half[...] = product(r.active.at[x], r.cotangent)
    incoming = [
        back.carried(b, r.device_decay[:, cut(b)], befores[b], r.back_totals, back_sems) for b in range(blocks)
    ]

    def half_copies():
        return (
            remote(r.active.at[1 - x], r.active_peer, r.half_send.at[0], r.half_recv.at[0], x_peer),
            remote(r.pre_grad.at[1 - y], r.pre_grad_peer, r.half_send.at[1], r.half_recv.at[1], y_peer),
        )

    for copy in half_copies():
        copy.start()

    @pl.when(y == 0)
    def _():
        wide_shares[0].across().start()

    @pl.when(x == 1)
    def _():
        query_copy().start()

    for b in range(blocks):
        decay, out_coef = r.decay[:, cut(b)], r.out_coef[:, cut(b)]
        skip = narrow(3)[:, features(b)]
        r.coef[:, cut(b)] = jnp.zeros_like(decay)
        r.slope[:, cut(b)] = jnp.zeros_like(decay)

        def chunk(i, adjoint, b=b, decay=decay, out_coef=out_coef, skip=skip):
            k = chunks - 1 - i
            base = pl.multiple_of(k * CHUNK, CHUNK)
            state = r.starts[k, :, cut(b)]
            for j in range(CHUNK):
                r.state[j] = state
                state = decay * state + r.rows[b, pl.ds(base + j, 1), :]
            coef, slope = r.coef[:, cut(b)], r.slope[:, cut(b)]
            for j in range(CHUNK - 1, -1, -1):
                adjoint = decay * adjoint + r.grad_rows[b, pl.ds(base + j, 1), :]
                r.part[j] = fold_states(out_coef * adjoint)
                coef = coef + adjoint * r.rows[b, pl.ds(base + j, 1), :]
                slope = slope + adjoint * r.state[j]
            r.coef[:, cut(b)] = coef
            r.slope[:, cut(b)] = slope
            rows = pl.ds(base, CHUNK)
            grad_mixed = jnp.sum(r.part[...], axis=1) + skip * r.grad[rows, cut(b)]
            r.shifted_grad[rows, cut(b)] = grad_mixed * r.value[rows, cut(b)]
            r.value_grad[rows, cut(b)] = grad_mixed * r.shifted[rows, cut(b)]
            return adjoint

        lax.fori_loop(0, chunks, chunk, incoming[b])
    store(r.value_grad, r.value_grad_hbm)

    def head_copy():
        return remote(
            r.shifted_grad.at[pl.ds(0, 8)], r.shifted_grad.at[pl.ds(tokens, 8)], r.halo_send.at[1], r.halo_recv.at[1], me - 1
        )

    @pl.when(jnp.logical_not(first))
    def _():
        head_copy().start()

    @pl.when(y == 1)
    def _():
        value_copy().start()

    for j in range(SHIFT):
        put(1 + j, over_tokens(r.shifted_grad[pl.ds(0, tokens), :] * r.keys[pl.ds(8 - j, tokens), :]))
    put(7, over_tokens(r.value_grad[...]))
    r.up_half[...] = product(r.normed2, r.pre_grad.at[y])

    @pl.when(last)
    def _():
        r.shifted_grad[pl.ds(tokens, 8), :] = jnp.zeros((8, width), F32)

    @pl.when(jnp.logical_not(last))
    def _():
        head_copy().wait_recv()

    key_grad = tap(0) * r.shifted_grad[pl.ds(0, tokens), :]
    for j in range(1, SHIFT):
        key_grad = key_grad + tap(j) * r.shifted_grad[pl.ds(j, tokens), :]
    r.key_grad[...] = key_grad
    store(r.key_grad, r.key_grad_hbm)

    @pl.when(x == 0)
    def _():
        key_copy().start()

    put(6, over_tokens(key_grad))

    for p in range(4):
        rows = pl.ds(p * small_start, small_start)
        coef = r.coef[rows, :]
        rate_grad = r.coef_rate[rows, :] * coef - r.decay[rows, :] * r.out_coef[rows, :] * r.slope[rows, :]
        step_grad = over_tokens(r.rate[rows, :] * rate_grad)
        put(8, step_grad if p == 0 else r.small[1, pl.ds(small_start + 4, 1), pl.ds(0, width)] + step_grad)
        r.small[p, pl.ds(0, small_start), pl.ds(0, width)] = narrow(4) * rate_grad
        r.small[p, pl.ds(0, small_start), pl.ds(width, width)] = r.in_coef[rows, :] * coef
    store(r.small, r.small_hbm)
    wide_shares[0].relay()

    cotangent_share.finish()
    normed2_share.finish()
    halves = half_copies()
    halves[0].wait()
    r.down_half[...] = r.down_half[...] + product(r.active_peer, r.cotangent_peer)
    store(r.down_half, r.down_half_hbm)
    halves[1].wait()
    r.up_half[...] = r.up_half[...] + product(r.normed2_peer, r.pre_grad_peer)
    store(r.up_half, r.up_half_hbm)
    normed1_share.finish()
    wide_shares[0].finish()
    key_copy().wait()
    gated_copy().wait()
    for copy in merged_copies + [normed_grad_copy, feed_copy]:
        copy.wait_send()
    ahead.drain(blocks, r.ends, r.totals, ahead_sems)
    back.drain(blocks, r.back_ends, r.back_totals, back_sems)

    @pl.when(jnp.logical_not(last))
    def _():
        halo_copy().wait_send()

    @pl.when(jnp.logical_not(first))
    def _():
        head_copy().wait_send()

    for copy in stores:
        copy.wait()


def front_call(span, inputs, in_hbm, outs, scratch, sems):
    names = [*inputs, *in_hbm, *outs, *scratch, *sems]
    results = pl.pallas_call(
        functools.partial(front_kernel, names, span),
        in_specs=[pl.BlockSpec(memory_space=pltpu.VMEM)] * len(inputs)
        + [pl.BlockSpec(memory_space=pltpu.HBM)] * len(in_hbm),
        out_specs=[pl.BlockSpec(memory_space=pltpu.HBM)] * len(outs),
        out_shape=[shape(*dims) for dims in outs.values()],
        scratch_shapes=[pltpu.VMEM(dims, F32) for dims in scratch.values()]
        + [pltpu.SemaphoreType.DMA(dims) for dims in sems.values()],
        compiler_params=pltpu.CompilerParams(collective_id=1, has_side_effects=True, vmem_limit_bytes=60 * 2**20),
        name="front",
    )(*inputs.values(), *in_hbm.values())
    return types.SimpleNamespace(**dict(zip(outs, results)))


MESH = pl.DeviceIdType.MESH


def is_far(i):
    return lax.rem(i, 5) == 2


class Plan:
    def __init__(self, feed_rows, mixer_rows, rows):
        self.rows = rows
        self.feed, self.mixer = feed_rows // rows, mixer_rows // 2 // rows
        self.small_rows = STATE // 4 + 8
        self.pieces = self.feed + self.mixer + -(-self.small_rows // rows)
        self.total = self.pieces * rows
        self.feed_rows, self.mixer_rows = feed_rows, mixer_rows


def sum_kernel(
    length, plan, lag,
    small_ref, gain_ref, up_half_ref, down_half_ref, normed_hbm, middle_grad_hbm, gated_hbm, query_grad_hbm, key_grad_hbm,
    value_grad_hbm, normed_x_hbm, narrow_x_hbm, wide_y_hbm, narrow_y_hbm, tokens_hbm, query_hbm, key_hbm, value_hbm,
    out_ref, input_grad_ref,
    normed_ref, middle_grad_ref, gated_ref, query_grad_ref, key_grad_ref, value_grad_ref,
    normed_x_ref, narrow_x_ref, wide_y_ref, narrow_y_ref, tokens_ref,
    sum_ref, got_ref, feed_got_ref, keep_ref, send_ref, mixer_got_ref, small_got_ref, small_sum_ref, weights_ref, local_ref,
    other_ref,
    load_sem, store_sem, chain_send, chain_recv, z_send, z_recv, side_send, side_recv, feed_send, feed_recv,
    mixer_send, mixer_recv, small_send, small_recv, core_send, core_recv
):
    me = lax.axis_index("seq")
    core = lax.axis_index("tp")
    place, quarter = me // 4, lax.rem(me, 4)
    x, y = lax.rem(quarter, 2), quarter // 2
    x_peer, y_peer = me + 1 - 2 * x, me + 2 - 4 * y
    quarter_x, quarter_y, quarter_d = quarter + 1 - 2 * x, quarter + 2 - 4 * y, 3 - quarter
    rows, pieces = plan.rows, plan.pieces
    width = gated_ref.shape[1]
    first = lag * (length - 1)
    spread = SPREAD
    started = (place, length - 1 - place)
    ahead = (me + 4, me - 4)
    behind = (me - 4, me + 4)
    side_peers = (x_peer, y_peer)
    side_bits = (x, y)
    halves = (up_half_ref, down_half_ref)
    barrier = pltpu.get_barrier_semaphore()

    def greet(peer):
        pl.semaphore_signal(barrier, inc=1, device_id={"seq": peer}, device_id_type=MESH)

    greet(x_peer)
    greet(y_peer)
    pl.semaphore_signal(barrier, inc=1, device_id={"tp": 1 - core}, device_id_type=MESH)
    pl.when(place > 0)(lambda: greet(me - 4))
    pl.when(place < length - 1)(lambda: greet(me + 4))
    pairs = [
        (half_ref.at[pl.ds(pl.multiple_of(bit * plan.feed_rows, 8), plan.feed_rows)], sum_ref.at[d, pl.ds(0, plan.feed_rows)])
        for d, (half_ref, bit) in enumerate(zip(halves, side_bits))
    ]
    pairs += [
        (normed_hbm, normed_ref),
        (query_grad_hbm, query_grad_ref),
        (key_grad_hbm, key_grad_ref),
        (normed_x_hbm, normed_x_ref),
        (narrow_x_hbm, narrow_x_ref),
        (gated_hbm, gated_ref),
        (value_grad_hbm, value_grad_ref),
        (middle_grad_hbm, middle_grad_ref),
        (wide_y_hbm, wide_y_ref),
        (narrow_y_hbm, narrow_y_ref),
        (tokens_hbm, tokens_ref),
        (query_hbm, weights_ref.at[0]),
        (key_hbm, weights_ref.at[1]),
        (value_hbm, weights_ref.at[2]),
    ]
    loads = [pltpu.make_async_copy(source, target, load_sem.at[n]) for n, (source, target) in enumerate(pairs)]
    for load in loads:
        load.start()
    pl.semaphore_wait(barrier, 3 + (place > 0).astype(jnp.int32) + (place < length - 1).astype(jnp.int32))

    def remote(source, target, send, recv, peer):
        return pltpu.make_async_remote_copy(
            src_ref=source,
            dst_ref=target,
            send_sem=send,
            recv_sem=recv,
            device_id={"seq": peer},
            device_id_type=MESH,
        )

    def at(i):
        return pl.ds(pl.multiple_of(i * rows, 8), rows)

    def feed_copy(d, i):
        source = pl.ds(pl.multiple_of((1 - side_bits[d]) * plan.feed_rows + i * rows, 8), rows)
        return remote(
            halves[d].at[source], feed_got_ref.at[d, at(i)], feed_send.at[d, i], feed_recv.at[d, i], side_peers[d]
        )

    def send_feed(i, _):
        for d in range(2):
            feed_copy(d, i).start()
        return 0

    lax.fori_loop(0, min(WINDOW, plan.feed), send_feed, 0)

    def features(ref, h):
        return ref[:, pl.ds(pl.multiple_of(h * width, LANES), width)]

    def query_or_key(h):
        narrow = jnp.where(x == 0, query_grad_ref[...], key_grad_ref[...])
        return dot(features(normed_ref, h), narrow, 0, 0) + dot(features(normed_x_ref, h), narrow_x_ref[...], 0, 0)

    def value_or_out(h):
        left = jnp.where(y == 0, features(normed_ref, h), gated_ref[...])
        right = jnp.where(y == 0, value_grad_ref[...], features(middle_grad_ref, h))
        wide, narrow = features(wide_y_ref, h), narrow_y_ref[...]
        return dot(left, right, 0, 0) + dot(jnp.where(y == 0, wide, narrow), jnp.where(y == 0, narrow, wide), 0, 0)

    mixer_copies = [
        remote(send_ref.at[n], mixer_got_ref.at[n], mixer_send.at[n], mixer_recv.at[n], peer)
        for n, peer in enumerate((y_peer, x_peer))
    ]
    for load in loads:
        load.wait()

    def send_mixer():
        send_ref[0] = query_or_key(1 - y)
        mixer_copies[0].start()
        send_ref[1] = value_or_out(1 - x)
        mixer_copies[1].start()


    def chain_copy(d, i):
        return remote(
            sum_ref.at[d, at(i)], got_ref.at[d, at(i)], chain_send.at[d, i], chain_recv.at[d, i], ahead[d]
        )

    def z_copy(d, i, k):
        ref = out_ref.at[(quarter, quarter_x, quarter_y, quarter_d)[k], d, at(i)]
        return remote(ref, ref, z_send.at[d, i, k], z_recv.at[d, i, k], behind[d])

    def side_copy(d, i, k):
        even = lax.rem(i, 2) == 0
        source = (quarter, quarter, jnp.where(even, quarter_x, quarter_y))[k]
        peer = (x_peer, y_peer, jnp.where(even, y_peer, x_peer))[k]
        ref = out_ref.at[source, d, at(i)]
        return remote(ref, ref, side_send.at[d, i, k], side_recv.at[d, i, k], peer)

    def chain_step(d, i):
        @pl.when(i < plan.feed)
        def _():
            feed_copy(d, i).wait_recv()
            sum_ref[d, at(i)] = sum_ref[d, at(i)] + feed_got_ref[d, at(i)]

        @pl.when(started[d] > 0)
        def _():
            chain_copy(d, i).wait_recv()
            sum_ref[d, at(i)] = sum_ref[d, at(i)] + got_ref[d, at(i)]

        @pl.when(started[d] < length - 1)
        def _():
            chain_copy(d, i).start()

        @pl.when(started[d] == length - 1)
        def _():
            store = pltpu.make_async_copy(sum_ref.at[d, at(i)], out_ref.at[quarter, d, at(i)], store_sem.at[d, i])
            store.start()
            store.wait()

    def kind(d, i):
        remaining = length - 1 - started[d]
        far = is_far(i)
        sideways = jnp.logical_or(jnp.logical_not(far), remaining == 0)
        onward = jnp.logical_and(far, remaining < length - 1)
        return remaining, sideways, onward

    def own_step(d, i):
        remaining, sideways, _ = kind(d, i)

        @pl.when(remaining > 0)
        def _():
            z_copy(d, i, 0).wait_recv()

        @pl.when(remaining < length - 1)
        def _():
            z_copy(d, i, 0).start()

        @pl.when(sideways)
        def _():
            side_copy(d, i, 0).start()
            side_copy(d, i, 1).start()

    def side_step(d, i):
        _, sideways, onward = kind(d, i)

        @pl.when(sideways)
        def _():
            side_copy(d, i, 0).wait_recv()
            side_copy(d, i, 1).wait_recv()
            side_copy(d, i, 2).start()

        @pl.when(jnp.logical_not(sideways))
        def _():
            z_copy(d, i, 1).wait_recv()
            z_copy(d, i, 2).wait_recv()

        @pl.when(onward)
        def _():
            z_copy(d, i, 1).start()
            z_copy(d, i, 2).start()

    def last_step(d, i):
        _, sideways, onward = kind(d, i)

        @pl.when(sideways)
        def _():
            side_copy(d, i, 2).wait_recv()

        @pl.when(jnp.logical_not(sideways))
        def _():
            z_copy(d, i, 3).wait_recv()

        @pl.when(onward)
        def _():
            z_copy(d, i, 3).start()

    def tick(t, _):
        @pl.when(t + WINDOW < plan.feed)
        def _():
            send_feed(t + WINDOW, 0)

        steps = ((chain_step, 0), (own_step, first), (last_step, first + 2 * spread), (side_step, first + spread))
        for step, late in steps:
            for d in range(2):
                passed = lag * started[d] if step is chain_step else spread * (length - 1 - started[d])
                i = t - late - passed
                pl.when(jnp.logical_and(i >= 0, i < pieces))(functools.partial(step, d, i))
        return 0

    core_copy = pltpu.make_async_remote_copy(
        src_ref=local_ref,
        dst_ref=other_ref,
        send_sem=core_send.at[0],
        recv_sem=core_recv.at[0],
        device_id={"tp": 1 - core},
        device_id_type=MESH,
    )
    small_x = remote(
        small_sum_ref.at[1 - x], small_got_ref.at[pl.ds(0, 2)], small_send.at[0], small_recv.at[0], x_peer
    )
    small_y = remote(
        small_sum_ref.at[x, 1 - y], small_got_ref.at[2], small_send.at[1], small_recv.at[1], y_peer
    )

    def normed_grad():
        local_ref[...] = (
            dot(query_grad_ref[...], weights_ref[0], 1, 1)
            + dot(key_grad_ref[...], weights_ref[1], 1, 1)
            + dot(value_grad_ref[...], weights_ref[2], 1, 1)
        )
        core_copy.start()

    def first_norm():
        core_copy.wait_recv()
        grad = local_ref[...] + other_ref[...]
        values = tokens_ref[...]
        centered = values - over_features(values)
        inverse = lax.rsqrt(over_features(centered * centered) + EPSILON)
        scaled = centered * inverse
        scaled_grad = grad * gain_ref[...].reshape(1, -1)
        scaled_grad = scaled_grad - over_features(scaled_grad) - scaled * over_features(scaled_grad * scaled)
        input_grad_ref[...] = middle_grad_ref[...] + inverse * scaled_grad
        for p in range(4):
            small_sum_ref[p // 2, p % 2] = small_ref[p]
        small_sum_ref[0, 0, pl.ds(STATE // 4, 1), :] = over_tokens(grad * scaled)
        small_sum_ref[0, 0, pl.ds(STATE // 4 + 1, 1), :] = over_tokens(grad)
        small_x.start()

    def keep_mixer():
        keep_ref[0] = query_or_key(y)
        keep_ref[1] = value_or_out(x)

    def add_small():
        small_x.wait()
        small_sum_ref[x] = small_sum_ref[x] + small_got_ref[pl.ds(0, 2)]
        small_y.start()

    def mixer_sums():
        for copy in mixer_copies:
            copy.wait_recv()
        count = plan.mixer_rows // 2
        for d in range(2):
            source, target = pl.ds(d * count, count), pl.ds(plan.feed_rows, count)
            for n in range(2):
                sum_ref[d, target, pl.ds(n * width, width)] = keep_ref[n, source, :] + mixer_got_ref[n, source, :]

    def small_sums():
        small_y.wait()
        start = plan.feed_rows + plan.mixer_rows // 2
        sum_ref[:, pl.ds(start, plan.total - start), :] = jnp.zeros((2, plan.total - start, sum_ref.shape[2]), F32)
        sum_ref[0, pl.ds(start, plan.small_rows), :] = small_sum_ref[x, y] + small_got_ref[2]

    stages = (
        (1, (send_mixer,)),
        (2, (normed_grad,)),
        (5, (first_norm,)),
        (8, (keep_mixer, add_small)),
        (plan.feed, (mixer_sums, small_sums)),
    )
    at_tick = 0
    for until, work in stages:
        lax.fori_loop(at_tick, until, tick, 0)
        at_tick = until
        for piece in work:
            piece()
    lax.fori_loop(at_tick, first + spread * (length + 1) + pieces, tick, 0)

    def drain(i, _):
        for d in range(2):
            remaining, sideways, onward = kind(d, i)
            pl.when(i < plan.feed)(lambda: feed_copy(d, i).wait_send())
            pl.when(remaining > 0)(lambda: chain_copy(d, i).wait_send())
            pl.when(remaining < length - 1)(lambda: z_copy(d, i, 0).wait_send())

            @pl.when(onward)
            def _():
                for k in range(1, 4):
                    z_copy(d, i, k).wait_send()

            @pl.when(sideways)
            def _():
                for k in range(3):
                    side_copy(d, i, k).wait_send()

        return 0

    lax.fori_loop(0, pieces, drain, 0)
    for copy in mixer_copies + [core_copy]:
        copy.wait_send()


def summed_quarters(plan, lag, args, in_hbm, collective_id):
    length = lax.axis_size("seq") // 4
    pieces, feed = plan.pieces, plan.feed
    tokens, columns = args[4].shape
    width = args[6].shape[1]
    sems = [(16,), (2, pieces), (2, pieces), (2, pieces), (2, pieces, 4), (2, pieces, 4), (2, pieces, 3), (2, pieces, 3)]
    sems += [(2, feed), (2, feed), (2,), (2,), (2,), (2,), (1,), (1,)]
    wide, narrow = (tokens, columns), (tokens, width)
    scratch = [wide, wide, narrow, narrow, narrow, narrow, wide, narrow, wide, narrow, wide]
    scratch += [(2, plan.total, columns)] * 2 + [(2, plan.feed_rows, columns)] + [(2, plan.mixer_rows, width)] * 3
    scratch += [(3, plan.small_rows, columns), (2, 2, plan.small_rows, columns), (3, columns, width)] + [(tokens, columns)] * 2
    return pl.pallas_call(
        functools.partial(sum_kernel, length, plan, lag),
        out_shape=[shape(4, 2, plan.total, columns), shape(tokens, columns)],
        in_specs=[pl.BlockSpec(memory_space=pltpu.HBM if n in in_hbm else pltpu.VMEM) for n in range(len(args))],
        out_specs=[pl.BlockSpec(memory_space=pltpu.HBM), pl.BlockSpec(memory_space=pltpu.VMEM)],
        scratch_shapes=[pltpu.VMEM(dims, F32) for dims in scratch] + [pltpu.SemaphoreType.DMA(dims) for dims in sems],
        compiler_params=pltpu.CompilerParams(
            collective_id=collective_id, has_side_effects=True, vmem_limit_bytes=60 * 2**20
        ),
        name="gradient_sums",
    )(*args)


def unpack_kernel(plan, sums_hbm, block_hbm, grad_hbm, *refs):
    (
        up_ref, down_ref, query_ref, key_ref, value_ref, out_ref, rate_ref, state_out_ref, block_out_ref, input_grad_ref,
        *vector_refs, sums_ref, rows_ref, load_sem, store_sem
    ) = refs
    columns, width = up_ref.shape[0], query_ref.shape[1]
    feed, count, state = plan.feed_rows, plan.mixer_rows // 2, STATE // 4
    loads, stores = [], []

    def load(source, target):
        loads.append(pltpu.make_async_copy(source, target, load_sem.at[len(loads)]))
        loads[-1].start()

    def store(source, target):
        stores.append(pltpu.make_async_copy(source, target, store_sem.at[len(stores)]))
        stores[-1].start()

    def span(start, size):
        return pl.ds(start, size)

    quarters = [(x, y, 2 * y + x) for x in range(2) for y in range(2)]
    for part in (span(feed, plan.total - feed), span(0, feed)):
        for _, _, q in quarters:
            for d in range(2):
                load(sums_hbm.at[q, d, part], sums_ref.at[q, d, part])
    load(block_hbm, rows_ref.at[0])
    load(grad_hbm, rows_ref.at[1])
    waiting = iter(loads)
    for x, y, q in quarters:
        for d in range(2):
            next(waiting).wait()
            mixer = sums_ref.at[q, d, span(feed, count)]
            target = (query_ref, key_ref)[x]
            store(mixer.at[:, span(0, width)], target.at[span((2 * y + d) * count, count)])
            if y == 0:
                target = value_ref.at[span((2 * x + d) * count, count)]
            else:
                target = out_ref.at[span(d * count, count), span(x * width, width)]
            store(mixer.at[:, span(width, width)], target)
        rows = span((2 * x + y) * state, state)
        last = sums_ref.at[q, 0, span(feed + count, state)]
        store(last.at[:, span(0, width)], rate_ref.at[rows])
        store(last.at[:, span(width, width)], state_out_ref.at[rows])
    for x, y, q in quarters:
        next(waiting).wait()
        store(sums_ref.at[q, 0, span(0, feed)], up_ref.at[span(x * feed, feed), span(y * columns, columns)])
        next(waiting).wait()
        store(sums_ref.at[q, 1, span(0, feed)], down_ref.at[span((2 * x + y) * feed, feed)])
    for n, target in enumerate((block_out_ref, input_grad_ref)):
        next(waiting).wait()
        store(rows_ref.at[n], target)
    *wide_refs, up_bias_ref, skip_ref, taps_ref, query_bias_ref, key_bias_ref, value_bias_ref, step_ref = vector_refs
    row = feed + count + state

    def narrow(k):
        return sums_ref[2, 0, row + k // 2, pl.ds(k % 2 * width, width)]

    for k, ref in enumerate(wide_refs):
        ref[...] = sums_ref[0, 0, row + k, :]
    for k in range(2):
        up_bias_ref[pl.ds(k * columns, columns)] = sums_ref[0, 0, row + 6 + k, :]
    for k in range(SHIFT):
        taps_ref[k, :] = narrow(1 + k)
    for k, ref in ((0, skip_ref), (5, query_bias_ref), (6, key_bias_ref), (7, value_bias_ref), (8, step_ref)):
        ref[...] = narrow(k)
    for item in stores:
        item.wait()


def unpacked(plan, args, matrices, vectors):
    return pl.pallas_call(
        functools.partial(unpack_kernel, plan),
        out_shape=[shape(*out.shape) for out in (*matrices, *args[1:], *vectors)],
        in_specs=[pl.BlockSpec(memory_space=pltpu.HBM)] * 3,
        out_specs=[pl.BlockSpec(memory_space=pltpu.HBM)] * (len(matrices) + 2)
        + [pl.BlockSpec(memory_space=pltpu.VMEM)] * len(vectors),
        scratch_shapes=[
            pltpu.VMEM(args[0].shape, F32),
            pltpu.VMEM((2, *args[1].shape), F32),
            pltpu.SemaphoreType.DMA((18,)),
            pltpu.SemaphoreType.DMA((34,)),
        ],
        compiler_params=pltpu.CompilerParams(vmem_limit_bytes=60 * 2**20),
        name="unpack",
    )(*args)


def on_device(
    tokens,
    cotangent,
    norm1_gain,
    norm1_bias,
    query_weight,
    query_bias,
    key_weight,
    key_bias,
    value_weight,
    value_bias,
    shift_kernel,
    log_step,
    state_rate,
    state_out,
    skip_gain,
    out_weight,
    out_bias,
    norm2_gain,
    norm2_bias,
    up_weight,
    up_bias,
    down_weight,
    down_bias,
):
    rows, columns = tokens.shape
    width = query_weight.shape[1]
    hidden = up_weight.shape[1]
    span = lax.axis_size("seq") // SEQS
    blocks, groups = width // LANES, span // 4
    plan = Plan(columns // 2, width, PIECE_ROWS)
    tok, wide_tok, state, row_blocks = (rows, width), (rows, columns), (STATE, width), (blocks, rows, LANES)
    hidden_tok = (rows, hidden // 2)
    ends, totals = (4, STATE, width), (groups, STATE, width)
    end_sems, total_sems = (blocks, 3), (blocks, max(1, groups - 1))
    front = front_call(
        span,
        dict(
            norm1_gain=norm1_gain,
            norm1_bias=norm1_bias,
            query_bias=query_bias,
            key_bias=key_bias,
            value_bias=value_bias,
            taps=shift_kernel,
            log_step=log_step,
            state_rate=state_rate,
            state_out=state_out,
            skip_gain=skip_gain,
            out_bias=out_bias,
            norm2_gain=norm2_gain,
            norm2_bias=norm2_bias,
            up_bias=up_bias,
            down_bias=down_bias,
        ),
        dict(
            tokens_hbm=tokens,
            key_hbm=key_weight,
            value_hbm=value_weight,
            query_hbm=query_weight,
            cotangent_hbm=cotangent,
            down_hbm=down_weight,
            out_hbm=out_weight,
            up_hbm=up_weight,
        ),
        dict(
            block_out_hbm=wide_tok,
            middle_grad_hbm=wide_tok,
            normed1_hbm=wide_tok,
            gated_hbm=tok,
            query_grad_hbm=tok,
            key_grad_hbm=tok,
            value_grad_hbm=tok,
            small_hbm=(4, plan.small_rows, columns),
            down_half_hbm=(hidden // 2, columns),
            up_half_hbm=(columns, hidden // 2),
            normed1_x=wide_tok,
            narrow_x=tok,
            wide_y=wide_tok,
            narrow_y=tok,
        ),
        dict(
            tokens=wide_tok,
            cotangent=wide_tok,
            key_weight=key_weight.shape,
            value_weight=value_weight.shape,
            query_weight=query_weight.shape,
            out_weight=out_weight.shape,
            up=up_weight.shape,
            down=down_weight.shape,
            normed1=wide_tok,
            keys=(rows + 8, width),
            value=tok,
            query=tok,
            shifted=tok,
            mixed=tok,
            out=tok,
            gated=tok,
            rows=row_blocks,
            grad_rows=row_blocks,
            starts=(rows // CHUNK, STATE, width),
            part=(CHUNK, 8, LANES),
            state=(CHUNK, STATE, LANES),
            ends=ends,
            totals=totals,
            back_ends=ends,
            back_totals=totals,
            merged=wide_tok,
            merged_other=wide_tok,
            middle=wide_tok,
            scaled=wide_tok,
            normed2=wide_tok,
            active=(2, *hidden_tok),
            pre_grad=(2, *hidden_tok),
            normed_grad=wide_tok,
            normed_grad_other=wide_tok,
            feed=wide_tok,
            feed_other=wide_tok,
            active_peer=hidden_tok,
            pre_grad_peer=hidden_tok,
            cotangent_peer=wide_tok,
            normed2_peer=wide_tok,
            middle_grad=wide_tok,
            gated_grad=tok,
            grad=tok,
            query_grad=tok,
            key_grad=tok,
            value_grad=tok,
            shifted_grad=(rows + 8, width),
            coef=state,
            slope=state,
            wide=(8, columns),
            narrow=(16, width),
            rate=state,
            decay=state,
            in_coef=state,
            out_coef=state,
            device_decay=state,
            coef_rate=state,
            small=(4, plan.small_rows, columns),
            block_out=wide_tok,
            down_half=(hidden // 2, columns),
            up_half=(columns, hidden // 2),
        ),
        dict(
            end_send=end_sems,
            end_recv=end_sems,
            total_send=total_sems,
            total_recv=total_sems,
            back_end_send=end_sems,
            back_end_recv=end_sems,
            back_total_send=total_sems,
            back_total_recv=total_sems,
            halo_send=(2,),
            halo_recv=(2,),
            load_sem=(8,),
            store_sem=(10,),
            core_send=(4,),
            core_recv=(4,),
            half_send=(4,),
            half_recv=(4,),
            share_send=(4, 2),
            share_recv=(4, 2),
        ),
    )
    sums, input_grad = summed_quarters(
        plan,
        LAG,
        (front.small_hbm, norm1_gain, front.up_half_hbm, front.down_half_hbm, front.normed1_hbm)
        + (front.middle_grad_hbm, front.gated_hbm, front.query_grad_hbm, front.key_grad_hbm, front.value_grad_hbm)
        + (front.normed1_x, front.narrow_x, front.wide_y, front.narrow_y, tokens, query_weight, key_weight, value_weight),
        range(2, 18),
        3,
    )
    (
        grad_up_weight,
        grad_down_weight,
        grad_query_weight,
        grad_key_weight,
        grad_value_weight,
        grad_out_weight,
        grad_state_rate,
        grad_state_out,
        block_out,
        input_grad,
        grad_norm1_gain,
        grad_norm1_bias,
        grad_norm2_gain,
        grad_norm2_bias,
        grad_out_bias,
        grad_down_bias,
        grad_up_bias,
        grad_skip_gain,
        grad_shift_kernel,
        grad_query_bias,
        grad_key_bias,
        grad_value_bias,
        grad_log_step,
    ) = unpacked(
        plan,
        (sums, front.block_out_hbm, input_grad),
        (up_weight, down_weight, query_weight, key_weight, value_weight, out_weight, state_rate, state_out),
        (norm1_gain, norm1_bias, norm2_gain, norm2_bias, out_bias, down_bias, up_bias, skip_gain, shift_kernel)
        + (query_bias, key_bias, value_bias, log_step),
    )
    return (
        block_out,
        input_grad,
        grad_norm1_gain,
        grad_norm1_bias,
        grad_query_weight,
        grad_query_bias,
        grad_key_weight,
        grad_key_bias,
        grad_value_weight,
        grad_value_bias,
        grad_shift_kernel,
        grad_log_step,
        grad_state_rate,
        grad_state_out,
        grad_skip_gain,
        grad_out_weight,
        grad_out_bias,
        grad_norm2_gain,
        grad_norm2_bias,
        grad_up_weight,
        grad_up_bias,
        grad_down_weight,
        grad_down_bias,
    )


def solution(mesh):
    return jax.shard_map(
        on_device,
        mesh=mesh,
        in_specs=(
            P("seq", None),
            P("seq", None),
            P(),
            P(),
            P(None, "tp"),
            P("tp"),
            P(None, "tp"),
            P("tp"),
            P(None, "tp"),
            P("tp"),
            P(None, "tp"),
            P("tp"),
            P(None, "tp"),
            P(None, "tp"),
            P("tp"),
            P("tp", None),
            P(),
            P(),
            P(),
            P(None, "tp"),
            P("tp"),
            P("tp", None),
            P(),
        ),
        out_specs=(
            P("seq", None),
            P("seq", None),
            P(),
            P(),
            P(None, "tp"),
            P("tp"),
            P(None, "tp"),
            P("tp"),
            P(None, "tp"),
            P("tp"),
            P(None, "tp"),
            P("tp"),
            P(None, "tp"),
            P(None, "tp"),
            P("tp"),
            P("tp", None),
            P(),
            P(),
            P(),
            P(None, "tp"),
            P("tp"),
            P("tp", None),
            P(),
        ),
        check_vma=False,
    )
```

time: 297 us -> 258 us (0.87)
  local copies, waits for them, and re-layouts: 19.7 us -> 0 us
  Pallas kernels: 270 us -> 257 us
  other arithmetic: 3.3 us -> 0 us
    unnamed x76 -> x0, local copies, waits for them, and re-layouts: 13.2 us -> none
    pallas_call x1, Pallas kernels: 176 us -> 165 us  [summed_quarters(): pl.pallas_call(functools.partial(sum_kernel, length, plan, lag), out_shap...]
    broadcast_in_dim x8 -> x0, local copies, waits for them, and re-layouts: 4.07 us -> none  [the longest x1 0.6 us: on_device(): up_bias[None]]
    pallas_call x3 -> x2, Pallas kernels: 93.3 us -> 92.3 us  [the longest x1 80.1 us: front_call(): pl.pallas_call(functools.partial(front_kernel, names, span), in_specs=[pl...]
where the time goes in v1:
time: 258 us
  Pallas kernels  257 us (100%)
    pallas_call x1, Pallas kernels, summed_quarters(): pl.pallas_call(functools.partial(sum_kernel, length, plan, lag), out_shap...  165 us
    pallas_call x1, Pallas kernels, front_call(): pl.pallas_call(functools.partial(front_kernel, names, span), in_specs=[pl...  80.1 us
    pallas_call x1, Pallas kernels, unpacked(): pl.pallas_call(functools.partial(unpack_kernel, plan), out_shape=[shape(*...  12.3 us

profile of v1, /device:TPU:0, one launch (start us, length us, event | category | flops | bytes accessed | tf_op | source)
XLA Modules:
  0.0 258.3 jit_solution(5486297763199879518)
XLA Ops:
  0.7 80.1 %front.1 = (f32[256,768]{1,0:T(8,128)}, f32[256,768]{1,0:T(8,128)}, f32[256,768]{1,0:T(8,128)}, f32[256,384]{1,0:T(8,128)}, f32[256,384]{1,0:T(8,128)}, /*index=...) custom-call(f32[768]{0:T(1024)} %gain_ref.1, ...), custom_call_target="tpu_custom_call" | custom-call | tf_op jit(solution)/shard_map/front/pallas_call | solution.py:611
  80.8 165.1 %gradient_sums.1 = (f32[4,2,600,768]{3,2,1,0:T(8,128)}, f32[256,768]{1,0:T(8,128)}) custom-call(f32[4,24,768]{2,1,0:T(8,128)} %get-tuple-element.62.small_ref, f32[768]{0:T(1024)} %gain_ref.1, f32[768,768]{1,0:T(8,128)} %get-tuple-element.63.up_half_ref, f32[768,768]{1,0:T(8,128)} %get-tuple-element.64.down_half_ref, ...), custom_call_target="tpu_custom_call" | custom-call | tf_op jit(solution)/shard_map/gradient_sums/pallas_call | solution.py:978
  245.8 12.3 %unpack.1 = (f32[768,1536]{1,0:T(8,128)}, f32[1536,768]{1,0:T(8,128)}, f32[768,384]{1,0:T(8,128)}, f32[768,384]{1,0:T(8,128)}, f32[768,384]{1,0:T(8,128)}, /*ind...) custom-call(f32[4,2,600,768]{3,2,1,0:T(8,128)} %get-tuple-element.75, ...), custom_call_target="tpu_custom_call" | custom-call | tf_op jit(solution)/shard_map/unpack/pallas_call | solution.py:1061

commit v2 on v1

--- a/solution.py
+++ b/solution.py
@@ -15,7 +15,9 @@
 CHUNK = 32
 PIECE_ROWS = 24
 LAG = 2
-SPREAD = 3
+SPREAD = 2
+SIDE = 4
+LAST = 6
 WINDOW = 3
 GELU_SCALE = (2.0 / 3.141592653589793) ** 0.5
 
@@ -323,16 +325,16 @@
         return remote(source, target, r.half_send.at[n], r.half_recv.at[n], peer)
 
     def key_copy():
-        return narrow_copy(r.key_grad, 2, r.narrow_x, x_peer)
+        return narrow_copy(r.key_grad, 4, r.narrow_x, x_peer)
 
     def query_copy():
-        return narrow_copy(r.query_grad, 2, r.narrow_x, x_peer)
+        return narrow_copy(r.query_grad, 4, r.narrow_x, x_peer)
 
     def gated_copy():
-        return narrow_copy(r.gated, 3, r.narrow_y, y_peer)
+        return narrow_copy(r.gated, 5, r.narrow_y, y_peer)
 
     def value_copy():
-        return narrow_copy(r.value_grad, 3, r.narrow_y, y_peer)
+        return narrow_copy(r.value_grad, 5, r.narrow_y, y_peer)
 
     cotangent_share.across().start()
 
@@ -414,8 +416,25 @@
             r.normed_grad[...] = normed_grad
         else:
             r.normed_grad[...] = r.normed_grad[...] + normed_grad
+    def half_copies(n):
+        rows = pl.ds(n * top, top)
+        return (
+            remote(
+                r.active.at[1 - x, rows], r.active_peer.at[rows], r.half_send.at[2 * n], r.half_recv.at[2 * n], x_peer
+            ),
+            remote(
+                r.pre_grad.at[1 - y, rows],
+                r.pre_grad_peer.at[rows],
+                r.half_send.at[2 * n + 1],
+                r.half_recv.at[2 * n + 1],
+                y_peer,
+            ),
+        )
+
     normed_grad_copy = core_copy(2, r.normed_grad, r.normed_grad_other)
     normed_grad_copy.start()
+    for copy in half_copies(0):
+        copy.start()
     for n in range(2):
         feed = dot(r.active[n], r.down[pl.ds(n * hidden_half, hidden_half), :], 1, 0)
         if n == 0:
@@ -457,6 +476,8 @@
             return adjoint
 
         back.send_end(b, lax.fori_loop(0, chunks, end, jnp.zeros_like(decay)), r.back_ends, back_sems)
+    for copy in half_copies(1):
+        copy.start()
     query_grad = r.gated_grad[...] * r.out[...]
     r.query_grad[...] = query_grad
     store(r.query_grad, r.query_grad_hbm)
@@ -480,24 +501,17 @@
         back.carried(b, r.device_decay[:, cut(b)], befores[b], r.back_totals, back_sems) for b in range(blocks)
     ]
 
-    def half_copies():
-        return (
-            remote(r.active.at[1 - x], r.active_peer, r.half_send.at[0], r.half_recv.at[0], x_peer),
-            remote(r.pre_grad.at[1 - y], r.pre_grad_peer, r.half_send.at[1], r.half_recv.at[1], y_peer),
-        )
-
-    for copy in half_copies():
-        copy.start()
-
-    @pl.when(y == 0)
-    def _():
-        wide_shares[0].across().start()
-
-    @pl.when(x == 1)
-    def _():
-        query_copy().start()
-
     for b in range(blocks):
+        if b == 1:
+
+            @pl.when(y == 0)
+            def _():
+                wide_shares[0].across().start()
+
+            @pl.when(x == 1)
+            def _():
+                query_copy().start()
+
         decay, out_coef = r.decay[:, cut(b)], r.out_coef[:, cut(b)]
         skip = narrow(3)[:, features(b)]
         r.coef[:, cut(b)] = jnp.zeros_like(decay)
@@ -578,11 +592,13 @@
 
     cotangent_share.finish()
     normed2_share.finish()
-    halves = half_copies()
-    halves[0].wait()
+    halves = half_copies(0) + half_copies(1)
+    for copy in halves[::2]:
+        copy.wait()
     r.down_half[...] = r.down_half[...] + product(r.active_peer, r.cotangent_peer)
     store(r.down_half, r.down_half_hbm)
-    halves[1].wait()
+    for copy in halves[1::2]:
+        copy.wait()
     r.up_half[...] = r.up_half[...] + product(r.normed2_peer, r.pre_grad_peer)
     store(r.up_half, r.up_half_hbm)
     normed1_share.finish()
@@ -626,7 +642,7 @@
 
 
 def is_far(i):
-    return lax.rem(i, 5) == 2
+    return lax.rem(i, 5) == 1
 
 
 class Plan:
@@ -854,7 +870,7 @@
         def _():
             send_feed(t + WINDOW, 0)
 
-        steps = ((chain_step, 0), (own_step, first), (last_step, first + 2 * spread), (side_step, first + spread))
+        steps = ((chain_step, 0), (own_step, first), (last_step, first + SIDE + LAST), (side_step, first + SIDE))
         for step, late in steps:
             for d in range(2):
                 passed = lag * started[d] if step is chain_step else spread * (length - 1 - started[d])
@@ -938,7 +954,7 @@
         at_tick = until
         for piece in work:
             piece()
-    lax.fori_loop(at_tick, first + spread * (length + 1) + pieces, tick, 0)
+    lax.fori_loop(at_tick, first + spread * (length - 1) + SIDE + LAST + pieces, tick, 0)
 
     def drain(i, _):
         for d in range(2):
@@ -1233,8 +1249,8 @@
             store_sem=(10,),
             core_send=(4,),
             core_recv=(4,),
-            half_send=(4,),
-            half_recv=(4,),
+            half_send=(6,),
+            half_recv=(6,),
             share_send=(4, 2),
             share_recv=(4, 2),
         ),

time: 258 us -> 254 us (0.984)
  Pallas kernels: 257 us -> 253 us
    pallas_call x1, Pallas kernels: 80.1 us -> 76.1 us  [front_call(): pl.pallas_call(functools.partial(front_kernel, names, span), in_specs=[pl...]
where the time goes in v2:
time: 254 us
  Pallas kernels  253 us (100%)
    pallas_call x1, Pallas kernels, summed_quarters(): pl.pallas_call(functools.partial(sum_kernel, length, plan, lag), out_shap...  165 us
    pallas_call x1, Pallas kernels, front_call(): pl.pallas_call(functools.partial(front_kernel, names, span), in_specs=[pl...  76.1 us
    pallas_call x1, Pallas kernels, unpacked(): pl.pallas_call(functools.partial(unpack_kernel, plan), out_shape=[shape(*...  12.3 us

profile of v2, /device:TPU:0, one launch (start us, length us, event | category | flops | bytes accessed | tf_op | source)
XLA Modules:
  0.0 254.3 jit_solution(3363430159520003138)
XLA Ops:
  0.7 76.1 %front.1 = (f32[256,768]{1,0:T(8,128)}, f32[256,768]{1,0:T(8,128)}, f32[256,768]{1,0:T(8,128)}, f32[256,384]{1,0:T(8,128)}, f32[256,384]{1,0:T(8,128)}, /*index=...) custom-call(f32[768]{0:T(1024)} %gain_ref.1, ...), custom_call_target="tpu_custom_call" | custom-call | tf_op jit(solution)/shard_map/front/pallas_call | solution.py:627
  76.8 165.1 %gradient_sums.1 = (f32[4,2,600,768]{3,2,1,0:T(8,128)}, f32[256,768]{1,0:T(8,128)}) custom-call(f32[4,24,768]{2,1,0:T(8,128)} %get-tuple-element.62.small_ref, f32[768]{0:T(1024)} %gain_ref.1, f32[768,768]{1,0:T(8,128)} %get-tuple-element.63.up_half_ref, f32[768,768]{1,0:T(8,128)} %get-tuple-element.64.down_half_ref, ...), custom_call_target="tpu_custom_call" | custom-call | tf_op jit(solution)/shard_map/gradient_sums/pallas_call | solution.py:994
  241.9 12.3 %unpack.1 = (f32[768,1536]{1,0:T(8,128)}, f32[1536,768]{1,0:T(8,128)}, f32[768,384]{1,0:T(8,128)}, f32[768,384]{1,0:T(8,128)}, f32[768,384]{1,0:T(8,128)}, /*ind...) custom-call(f32[4,2,600,768]{3,2,1,0:T(8,128)} %get-tuple-element.75, ...), custom_call_target="tpu_custom_call" | custom-call | tf_op jit(solution)/shard_map/unpack/pallas_call | solution.py:1077

commit v3 on v2

--- a/solution.py
+++ b/solution.py
@@ -19,6 +19,7 @@
 SIDE = 4
 LAST = 6
 WINDOW = 3
+EARLY = 2
 GELU_SCALE = (2.0 / 3.141592653589793) ** 0.5
 
 EPSILON = 1e-05
@@ -298,14 +299,13 @@
         ahead.send_end(b, lax.fori_loop(0, chunks, scan, jnp.zeros_like(decay)), r.ends, ahead_sems)
     loads[3].wait()
     r.query[...] = dot(r.normed1[...], r.query_weight[...], 1, 0) + narrow(0)
-    befores = [ahead.group_total(b, r.device_decay[:, cut(b)], r.ends, r.totals, ahead_sems) for b in range(blocks)]
     loads[4].wait()
     loads[5].wait()
-    for n in range(2):
-        r.pre_grad[n] = dot(r.cotangent[...], r.down[pl.ds(n * hidden_half, hidden_half), :], 1, 1)
-    incoming = [
-        ahead.carried(b, r.device_decay[:, cut(b)], befores[b], r.totals, ahead_sems) for b in range(blocks)
-    ]
+    befores = []
+    for b in range(blocks):
+        befores.append(ahead.group_total(b, r.device_decay[:, cut(b)], r.ends, r.totals, ahead_sems))
+        if b < 2:
+            r.pre_grad[b] = dot(r.cotangent[...], r.down[pl.ds(b * hidden_half, hidden_half), :], 1, 1)
 
     cotangent_share = Share(
         ahead, r.cotangent, r.cotangent_peer, r.share_send.at[0], r.share_recv.at[0], x_peer, core, other_core
@@ -358,7 +358,8 @@
             r.gated[rows, cut(b)] = r.query[rows, cut(b)] * out
             return state
 
-        lax.fori_loop(0, chunks, carry, incoming[b])
+        incoming = ahead.carried(b, r.device_decay[:, cut(b)], befores[b], r.totals, ahead_sems)
+        lax.fori_loop(0, chunks, carry, incoming)
     store(r.gated, r.gated_hbm)
 
     def core_copy(n, source, target):
@@ -411,13 +412,10 @@
         pre_grad = r.pre_grad[n] * slope
         r.pre_grad[n] = pre_grad
         r.small[0, pl.ds(small_start + 6 + n, 1), :] = over_tokens(pre_grad)
-        normed_grad = dot(pre_grad, r.up[:, part], 1, 1)
-        if n == 0:
-            r.normed_grad[...] = normed_grad
-        else:
-            r.normed_grad[...] = r.normed_grad[...] + normed_grad
+    early = tokens * EARLY // 8
+
     def half_copies(n):
-        rows = pl.ds(n * top, top)
+        rows = (pl.ds(0, early), pl.ds(early, tokens - early))[n]
         return (
             remote(
                 r.active.at[1 - x, rows], r.active_peer.at[rows], r.half_send.at[2 * n], r.half_recv.at[2 * n], x_peer
@@ -431,10 +429,12 @@
             ),
         )
 
+    for copy in half_copies(0):
+        copy.start()
+    r.normed_grad[...] = dot(r.pre_grad[0], r.up[:, pl.ds(0, hidden_half)], 1, 1)
+    r.normed_grad[...] = r.normed_grad[...] + dot(r.pre_grad[1], r.up[:, pl.ds(hidden_half, hidden_half)], 1, 1)
     normed_grad_copy = core_copy(2, r.normed_grad, r.normed_grad_other)
     normed_grad_copy.start()
-    for copy in half_copies(0):
-        copy.start()
     for n in range(2):
         feed = dot(r.active[n], r.down[pl.ds(n * hidden_half, hidden_half), :], 1, 0)
         if n == 0:
@@ -497,9 +497,6 @@
         return dot(left_ref[...], right_ref[...], 0, 0)
 
     r.down_half[...] = product(r.active.at[x], r.cotangent)
-    incoming = [
-        back.carried(b, r.device_decay[:, cut(b)], befores[b], r.back_totals, back_sems) for b in range(blocks)
-    ]
 
     for b in range(blocks):
         if b == 1:
@@ -538,7 +535,8 @@
             r.value_grad[rows, cut(b)] = grad_mixed * r.shifted[rows, cut(b)]
             return adjoint
 
-        lax.fori_loop(0, chunks, chunk, incoming[b])
+        incoming = back.carried(b, r.device_decay[:, cut(b)], befores[b], r.back_totals, back_sems)
+        lax.fori_loop(0, chunks, chunk, incoming)
     store(r.value_grad, r.value_grad_hbm)
 
     def head_copy():

time: 254 us -> 249 us (0.980)
  Pallas kernels: 253 us -> 248 us
    pallas_call x1, Pallas kernels: 76.1 us -> 71.6 us  [front_call(): pl.pallas_call(functools.partial(front_kernel, names, span), in_specs=[pl...]
where the time goes in v3:
time: 249 us
  Pallas kernels  248 us (100%)
    pallas_call x1, Pallas kernels, summed_quarters(): pl.pallas_call(functools.partial(sum_kernel, length, plan, lag), out_shap...  164 us
    pallas_call x1, Pallas kernels, front_call(): pl.pallas_call(functools.partial(front_kernel, names, span), in_specs=[pl...  71.6 us
    pallas_call x1, Pallas kernels, unpacked(): pl.pallas_call(functools.partial(unpack_kernel, plan), out_shape=[shape(*...  12.3 us

profile of v3, /device:TPU:0, one launch (start us, length us, event | category | flops | bytes accessed | tf_op | source)
XLA Modules:
  0.0 248.8 jit_solution(6642137799468439995)
XLA Ops:
  0.7 71.6 %front.1 = (f32[256,768]{1,0:T(8,128)}, f32[256,768]{1,0:T(8,128)}, f32[256,768]{1,0:T(8,128)}, f32[256,384]{1,0:T(8,128)}, f32[256,384]{1,0:T(8,128)}, /*index=...) custom-call(f32[768]{0:T(1024)} %gain_ref.1, ...), custom_call_target="tpu_custom_call" | custom-call | tf_op jit(solution)/shard_map/front/pallas_call | solution.py:625
  72.3 164.0 %gradient_sums.1 = (f32[4,2,600,768]{3,2,1,0:T(8,128)}, f32[256,768]{1,0:T(8,128)}) custom-call(f32[4,24,768]{2,1,0:T(8,128)} %get-tuple-element.62.small_ref, f32[768]{0:T(1024)} %gain_ref.1, f32[768,768]{1,0:T(8,128)} %get-tuple-element.63.up_half_ref, f32[768,768]{1,0:T(8,128)} %get-tuple-element.64.down_half_ref, ...), custom_call_target="tpu_custom_call" | custom-call | tf_op jit(solution)/shard_map/gradient_sums/pallas_call | solution.py:992
  236.3 12.3 %unpack.1 = (f32[768,1536]{1,0:T(8,128)}, f32[1536,768]{1,0:T(8,128)}, f32[768,384]{1,0:T(8,128)}, f32[768,384]{1,0:T(8,128)}, f32[768,384]{1,0:T(8,128)}, /*ind...) custom-call(f32[4,2,600,768]{3,2,1,0:T(8,128)} %get-tuple-element.75, ...), custom_call_target="tpu_custom_call" | custom-call | tf_op jit(solution)/shard_map/unpack/pallas_call | solution.py:1075

commit v4 on v3

--- a/solution.py
+++ b/solution.py
@@ -650,6 +650,7 @@
         self.small_rows = STATE // 4 + 8
         self.pieces = self.feed + self.mixer + -(-self.small_rows // rows)
         self.total = self.pieces * rows
+        self.counts = (self.pieces, self.feed + self.mixer)
         self.feed_rows, self.mixer_rows = feed_rows, mixer_rows
 
 
@@ -873,7 +874,7 @@
             for d in range(2):
                 passed = lag * started[d] if step is chain_step else spread * (length - 1 - started[d])
                 i = t - late - passed
-                pl.when(jnp.logical_and(i >= 0, i < pieces))(functools.partial(step, d, i))
+                pl.when(jnp.logical_and(i >= 0, i < plan.counts[d]))(functools.partial(step, d, i))
         return 0
 
     core_copy = pltpu.make_async_remote_copy(
@@ -954,26 +955,26 @@
             piece()
     lax.fori_loop(at_tick, first + spread * (length - 1) + SIDE + LAST + pieces, tick, 0)
 
-    def drain(i, _):
-        for d in range(2):
-            remaining, sideways, onward = kind(d, i)
-            pl.when(i < plan.feed)(lambda: feed_copy(d, i).wait_send())
-            pl.when(remaining > 0)(lambda: chain_copy(d, i).wait_send())
-            pl.when(remaining < length - 1)(lambda: z_copy(d, i, 0).wait_send())
-
-            @pl.when(onward)
-            def _():
-                for k in range(1, 4):
-                    z_copy(d, i, k).wait_send()
-
-            @pl.when(sideways)
-            def _():
-                for k in range(3):
-                    side_copy(d, i, k).wait_send()
+    def drain(d, i, _):
+        remaining, sideways, onward = kind(d, i)
+        pl.when(i < plan.feed)(lambda: feed_copy(d, i).wait_send())
+        pl.when(remaining > 0)(lambda: chain_copy(d, i).wait_send())
+        pl.when(remaining < length - 1)(lambda: z_copy(d, i, 0).wait_send())
+
+        @pl.when(onward)
+        def _():
+            for k in range(1, 4):
+                z_copy(d, i, k).wait_send()
+
+        @pl.when(sideways)
+        def _():
+            for k in range(3):
+                side_copy(d, i, k).wait_send()
 
         return 0
 
-    lax.fori_loop(0, pieces, drain, 0)
+    for d in range(2):
+        lax.fori_loop(0, plan.counts[d], functools.partial(drain, d), 0)
     for copy in mixer_copies + [core_copy]:
         copy.wait_send()
 
@@ -1023,9 +1024,10 @@
         return pl.ds(start, size)
 
     quarters = [(x, y, 2 * y + x) for x in range(2) for y in range(2)]
-    for part in (span(feed, plan.total - feed), span(0, feed)):
+    for start in (feed, 0):
         for _, _, q in quarters:
             for d in range(2):
+                part = span(start, plan.counts[d] * plan.rows - feed if start else feed)
                 load(sums_hbm.at[q, d, part], sums_ref.at[q, d, part])
     load(block_hbm, rows_ref.at[0])
     load(grad_hbm, rows_ref.at[1])

time: 249 us -> 249 us (level)
  no operation moved by 1% of the time
where the time goes in v4:
time: 249 us
  Pallas kernels  248 us (100%)
    pallas_call x1, Pallas kernels, summed_quarters(): pl.pallas_call(functools.partial(sum_kernel, length, plan, lag), out_shap...  164 us
    pallas_call x1, Pallas kernels, front_call(): pl.pallas_call(functools.partial(front_kernel, names, span), in_specs=[pl...  71.6 us
    pallas_call x1, Pallas kernels, unpacked(): pl.pallas_call(functools.partial(unpack_kernel, plan), out_shape=[shape(*...  12.3 us

profile of v4, /device:TPU:0, one launch (start us, length us, event | category | flops | bytes accessed | tf_op | source)
XLA Modules:
  0.0 249.1 jit_solution(13634090070402955646)
XLA Ops:
  0.7 71.6 %front.1 = (f32[256,768]{1,0:T(8,128)}, f32[256,768]{1,0:T(8,128)}, f32[256,768]{1,0:T(8,128)}, f32[256,384]{1,0:T(8,128)}, f32[256,384]{1,0:T(8,128)}, /*index=...) custom-call(f32[768]{0:T(1024)} %gain_ref.1, ...), custom_call_target="tpu_custom_call" | custom-call | tf_op jit(solution)/shard_map/front/pallas_call | solution.py:625
  72.3 164.3 %gradient_sums.1 = (f32[4,2,600,768]{3,2,1,0:T(8,128)}, f32[256,768]{1,0:T(8,128)}) custom-call(f32[4,24,768]{2,1,0:T(8,128)} %get-tuple-element.62.small_ref, f32[768]{0:T(1024)} %gain_ref.1, f32[768,768]{1,0:T(8,128)} %get-tuple-element.63.up_half_ref, f32[768,768]{1,0:T(8,128)} %get-tuple-element.64.down_half_ref, ...), custom_call_target="tpu_custom_call" | custom-call | tf_op jit(solution)/shard_map/gradient_sums/pallas_call | solution.py:993
  236.6 12.3 %unpack.1 = (f32[768,1536]{1,0:T(8,128)}, f32[1536,768]{1,0:T(8,128)}, f32[768,384]{1,0:T(8,128)}, f32[768,384]{1,0:T(8,128)}, f32[768,384]{1,0:T(8,128)}, /*ind...) custom-call(f32[4,2,600,768]{3,2,1,0:T(8,128)} %get-tuple-element.75, ...), custom_call_target="tpu_custom_call" | custom-call | tf_op jit(solution)/shard_map/unpack/pallas_call | solution.py:1077
